TPU v7x, 32 devices: a whole 2x2x4 slice. The times are simulated.
32 devices in a mesh: groups: 2 (over x), box: 16 (over z, y, core).
Axes of the slice: x: 2, y: 2, z: 4, core: 2. Of those that a mesh axis runs over, the one named last changes fastest.
Arguments:
- coeffs: bfloat16 [4, 64, 65536], P(None, None, ('groups', 'box')), parts along dimension 2, may hold values from -6 to 6
- operators: bfloat16 [4, 8, 64, 128], replicated, may hold values from -0.5 to 0.5
- pattern: int32 [4, 65536], P(None, 'groups'), parts along dimension 1, may hold values from 0 to 7
- owner_order: int32 [65536], P(('groups', 'box')), parts along dimension 0, may hold values from 0 to 2047, as said below
Outputs:
- targets: bfloat16 [4, 64, 65536], P(None, None, ('groups', 'box')), parts along dimension 2
There are 2 independent parts, one for each index of `groups`. A program takes and returns all parts, laid end to end along the dimension named above; an argument that names none is the same for every part. Nothing has to cross between parts.
Inputs may be any that keep to these rules, and one draw needn't show every extreme that they name: `owner_order`: each aligned block of 2048 entries is a permutation of 0 .. 2047.
All inputs are finite; a program needn't handle non-finite values.
Results may differ from a plain program's by a relative error of at most 0.0066.
Values may be sent and summed in bfloat16 or wider, within the bound.
No kernel may reach another device: no remote copies, remote signals or barrier semaphores. Data moves between devices by JAX's collectives and lax.ppermute only.
A program may use at most 64 MiB of HBM per device.

v0:
```python
import jax
import jax.numpy as jnp
from jax import lax
from jax.sharding import PartitionSpec as P


def from_partner(block, axis, distance):
    count = lax.axis_size(axis)
    route = []
    for low in range(count):
        high = low | 1 << distance
        if high != low and high < count:
            route += [(low, high), (high, low)]
    return lax.ppermute(block, axis, route)


def body(coeffs, operators, pattern, owner_order):
    device_count = lax.axis_size("box")
    device_index = lax.axis_index("box")
    bit_count = device_count.bit_length() - 1
    local_boxes = coeffs.shape[2]
    rank_count = coeffs.shape[1]
    level_count = operators.shape[0]
    own_picks = lax.dynamic_slice_in_dim(pattern, device_index * local_boxes, local_boxes, 1)
    state = coeffs
    for level_index in range(level_count):
        bit_index = bit_count - 1 - level_index
        parity = device_index >> bit_index & 1
        matrices = operators[level_index]
        first_part = matrices[:, :, :rank_count]
        second_part = matrices[:, :, rank_count:]
        own_matrices = jnp.where(parity == 0, first_part, second_part)
        far_matrices = jnp.where(parity == 0, second_part, first_part)
        partner_state = from_partner(state, "box", bit_index)
        choose_row = own_picks[level_index].reshape(1, 1, local_boxes)
        updated = jnp.zeros(state.shape, jnp.float32)
        for table_index in range(matrices.shape[0]):
            term = jnp.einsum(
                "oi,sib->sob", own_matrices[table_index], state, preferred_element_type=jnp.float32
            )
            term = term + jnp.einsum(
                "oi,sib->sob",
                far_matrices[table_index],
                partner_state,
                preferred_element_type=jnp.float32,
            )
            updated = updated + jnp.where(choose_row == table_index, term, 0.0)
        state = updated.astype(jnp.bfloat16)
    relaid = lax.all_to_all(state, "box", split_axis=2, concat_axis=2, tiled=True)
    return jnp.take(relaid, owner_order, axis=2)


def solution(mesh):
    return jax.shard_map(
        body,
        mesh=mesh,
        in_specs=(P(None, None, ("groups", "box")), P(), P(None, "groups"), P(("groups", "box"))),
        out_specs=P(None, None, ("groups", "box")),
        check_vma=False,
    )
```

profile of v0, /device:TPU:0, one launch (start us, length us, event | category | flops | bytes accessed | tf_op | source)
XLA Modules:
  0.0 183.0 jit_solution(15411041910931538547)
XLA Ops:
  0.0 4.0 %collective-permute-start = (bf16[4,64,2048]{2,1,0:T(8,128)(2,1)}, bf16[4,64,2048]{2,1,0:T(8,128)(2,1)S(1)}, u32[]{:S(2)}, u32[]{:S(2)}) collective-permute-start(bf16[4,64,2048]{2,1,0:T(8,128)(2,1)} %param.4), channel_id=1, source_target_pairs={{0,8},{8,0},{1,9},{9,1},{2,10},{10,2},{3,11},{11,3},{4,12},{12,4},... | collective-permute-start | bytes 3145736 | tf_op jit(solution)/shard_map/ppermute | solution.py:14
  4.0 1.1 slice_bitcast_fusion
  5.3 1.8 fusion.96
  7.1 1.7 fusion.95
  8.8 1.7 fusion.94
  10.5 1.8 fusion.93
  12.3 1.8 fusion.92
  14.3 1.7 compare_reduce_fusion
  17.4 32.5 %collective-permute-done = bf16[4,64,2048]{2,1,0:T(8,128)(2,1)S(1)} collective-permute-done((bf16[4,64,2048]{2,1,0:T(8,128)(2,1)}, bf16[4,64,2048]{2,1,0:T(8,128)(2,1)S(1)}, u32[]{:S(2)}, u32[]{:S(2)}) %collective-permute-start) | collective-permute-done | bytes 1048608 | tf_op jit(solution)/shard_map/ppermute | solution.py:14
  50.4 1.2 copy-done.5
  52.0 1.1 copy-done.4
  53.1 0.5 fusion.56
  53.6 1.1 copy-done.3
  55.2 1.1 copy-done.2
  56.3 0.5 fusion.52
  56.8 0.5 fusion.50
  57.3 0.5 fusion.48
  57.8 0.5 fusion.67
  58.3 0.8 collective-permute-start.1
  62.5 20.2 %collective-permute-done.1 = bf16[4,64,2048]{2,1,0:T(8,128)(2,1)S(1)} collective-permute-done((bf16[4,64,2048]{2,1,0:T(8,128)(2,1)S(1)}, bf16[4,64,2048]{2,1,0:T(8,128)(2,1)S(1)}, u32[]{:S(2)}, u32[]{:S(2)}) %collective-permute-start.1) | collective-permute-done | bytes 1048608 | tf_op jit(solution)/shard_map/ppermute | solution.py:14
  84.0 0.6 fusion.39
  86.5 1.3 collective-permute-start.2
  91.1 18.8 %collective-permute-done.2 = bf16[4,64,2048]{2,1,0:T(8,128)(2,1)S(1)} collective-permute-done((bf16[4,64,2048]{2,1,0:T(8,128)(2,1)S(1)}, bf16[4,64,2048]{2,1,0:T(8,128)(2,1)S(1)}, u32[]{:S(2)}, u32[]{:S(2)}) %collective-permute-start.2) | collective-permute-done | bytes 1048608 | tf_op jit(solution)/shard_map/ppermute | solution.py:14
  117.9 0.7 fusion.11
  120.8 1.4 copy.7
  122.2 2.2 %reshape.398 = bf16[16,2,16384]{2,1,0:T(2,128)(2,1)} reshape(bf16[2048,4,64]{2,1,0:T(4,128)(2,1)S(1)} %bitcast.340) | data formatting | bytes 2097152
  124.4 7.4 %all-to-all-start = ((bf16[16,2,16384]{2,1,0:T(2,128)(2,1)}), bf16[16,2,16384]{2,1,0:T(2,128)(2,1)S(1)}, u32[]{:S(2)}, u32[]{:S(2)}) async-start(bf16[16,2,16384]{2,1,0:T(2,128)(2,1)} %reshape.398), calls=%async_computation | async-start | bytes 2097152 | tf_op jit(solution)/shard_map/all_to_all | solution.py:49
  131.9 22.9 %all-to-all-done = bf16[16,2,16384]{2,1,0:T(2,128)(2,1)S(1)} async-done(((bf16[16,2,16384]{2,1,0:T(2,128)(2,1)}), bf16[16,2,16384]{2,1,0:T(2,128)(2,1)S(1)}, u32[]{:S(2)}, u32[]{:S(2)}) %all-to-all-start) | async-done | bytes 1048608 | tf_op jit(solution)/shard_map/all_to_all | solution.py:49
  154.8 1.3 reshape.399
  156.2 14.5 %gather_fusion = bf16[2048,4,64]{2,1,0:T(4,128)(2,1)} fusion(bf16[4,64,2048]{1,0,2:T(4,128)(2,1)S(1)} %bitcast.341, s32[2048]{0:T(1024)S(1)} %fusion.100), kind=kCustom, calls=%fused_computation | custom fusion | bytes 2105344 | tf_op jit(solution)/shard_map/jit(_take)/gather | solution.py:50
  170.7 10.0 %select_bitcast_fusion = bf16[4,64,2048]{1,0,2:T(4,128)(2,1)S(1)} fusion(bf16[2048,4,64]{2,1,0:T(4,128)(2,1)} %gather_fusion, pred[2048]{0:T(1024)(128)(4,1)S(1)} %compare_and_fusion), kind=kLoop, calls=%fused_computation.101 | loop fusion | flops 524288 | bytes 2099200 | tf_op jit(solution)/shard_map/jit(_take)/select_n | solution.py:50
  180.7 2.3 %copy.8 = bf16[4,64,2048]{2,1,0:T(8,128)(2,1)} copy(bf16[4,64,2048]{1,0,2:T(4,128)(2,1)S(1)} %select_bitcast_fusion) | data formatting | bytes 2097152 | tf_op jit(solution)/shard_map/jit(_take)/select_n | solution.py:50
  (70 shorter events, 22.7 us)
Async XLA Ops:
  0.0 5.3 %copy-start = (bf16[4,64,2048]{2,1,0:T(8,128)(2,1)S(1)}, bf16[4,64,2048]{2,1,0:T(8,128)(2,1)}, u32[]{:S(2)}) copy-start(bf16[4,64,2048]{2,1,0:T(8,128)(2,1)} %param.4) | copy-start | bytes 3145732
  0.0 49.9 %collective-permute-start = (bf16[4,64,2048]{2,1,0:T(8,128)(2,1)}, bf16[4,64,2048]{2,1,0:T(8,128)(2,1)S(1)}, u32[]{:S(2)}, u32[]{:S(2)}) collective-permute-start(bf16[4,64,2048]{2,1,0:T(8,128)(2,1)} %param.4), channel_id=1, source_target_pairs={{0,8},{8,0},{1,9},{9,1},{2,10},{10,2},{3,11},{11,3},{4,12},{12,4},... | collective-permute-start | bytes 3145736 | tf_op jit(solution)/shard_map/ppermute | solution.py:14
  17.0 32.9 %copy-start.1 = (f32[64,4,2048]{2,0,1:T(8,128)S(1)}, f32[64,4,2048]{2,0,1:T(8,128)}, u32[]{:S(2)}) copy-start(f32[64,4,2048]{2,0,1:T(8,128)} %fusion.96) | copy-start | bytes 6291460
  50.0 1.6 copy-start.5
  51.5 1.6 copy-start.4
  53.1 1.6 copy-start.3
  54.7 1.6 copy-start.2
  58.3 24.4 %collective-permute-start.1 = (bf16[4,64,2048]{2,1,0:T(8,128)(2,1)S(1)}, bf16[4,64,2048]{2,1,0:T(8,128)(2,1)S(1)}, u32[]{:S(2)}, u32[]{:S(2)}) collective-permute-start(bf16[4,64,2048]{2,1,0:T(8,128)(2,1)S(1)} %fusion.67), channel_id=1, source_target_pairs={{0,4},{4,0},{1,5},{5,1},{2,6},{6,2},{3,7},{7,3},{8,12},{12,8},{9,1... | collective-permute-start | bytes 3145736 | tf_op jit(solution)/shard_map/ppermute | solution.py:14
  86.5 23.5 %collective-permute-start.2 = (bf16[4,64,2048]{2,1,0:T(8,128)(2,1)S(1)}, bf16[4,64,2048]{2,1,0:T(8,128)(2,1)S(1)}, u32[]{:S(2)}, u32[]{:S(2)}) collective-permute-start(bf16[4,64,2048]{2,1,0:T(8,128)(2,1)S(1)} %fusion.66), channel_id=1, source_target_pairs={{0,2},{2,0},{1,3},{3,1},{4,6},{6,4},{5,7},{7,5},{8,10},{10,8},{9,1... | collective-permute-start | bytes 3145736 | tf_op jit(solution)/shard_map/ppermute | solution.py:14
  113.5 3.4 %collective-permute-start.3 = (bf16[4,64,2048]{2,1,0:T(8,128)(2,1)S(1)}, bf16[4,64,2048]{2,1,0:T(8,128)(2,1)S(1)}, u32[]{:S(2)}, u32[]{:S(2)}) collective-permute-start(bf16[4,64,2048]{2,1,0:T(8,128)(2,1)S(1)} %fusion.65), channel_id=1, source_target_pairs={{0,1},{1,0},{2,3},{3,2},{4,5},{5,4},{6,7},{7,6},{8,9},{9,8},{10,11... | collective-permute-start | bytes 3145736 | tf_op jit(solution)/shard_map/ppermute | solution.py:14
  122.2 9.7 %copy-start.6 = (s32[2048]{0:T(1024)S(1)}, s32[2048]{0:T(1024)}, u32[]{:S(2)}) copy-start(s32[2048]{0:T(1024)} %param.7) | copy-start | bytes 24580
  124.4 30.4 %all-to-all-start = ((bf16[16,2,16384]{2,1,0:T(2,128)(2,1)}), bf16[16,2,16384]{2,1,0:T(2,128)(2,1)S(1)}, u32[]{:S(2)}, u32[]{:S(2)}) async-start(bf16[16,2,16384]{2,1,0:T(2,128)(2,1)} %reshape.398), calls=%async_computation | async-start | bytes 2097152 | tf_op jit(solution)/shard_map/all_to_all | solution.py:49
where the time goes:
time: 185 us; the launch traced here: 183 us
  waiting for transfers between devices  94.5 us (51%)
  matrix products  34.7 us (19%)
  local copies, waits for them, and re-layouts  27.4 us (15%)
  starting transfers between devices  13.7 us (7%)
  other arithmetic  12.2 us (7%)
    ppermute x4, waiting for transfers between devices, from_partner(): return lax.ppermute(block, axis, route)  71.6 us
    all_to_all x1, waiting for transfers between devices, body(): lax.all_to_all(state, 'box', split_axis=2, concat_axis=2, tiled=True)  22.9 us
    dot_general x32, matrix products, body(): jnp.einsum('oi,sib->sob', own_matrices[table_index], state, preferred_ele...  20 us
    dot_general x32, matrix products, body(): jnp.einsum('oi,sib->sob', far_matrices[table_index], partner_state, prefe...  14.8 us
    gather x1, local copies, waits for them, and re-layouts, body(): return jnp.take(relaid, owner_order, axis=2)  14.5 us
    select_n x1, other arithmetic, body(): return jnp.take(relaid, owner_order, axis=2)  10 us
    unnamed x16, local copies, waits for them, and re-layouts  8.07 us
    all_to_all x1, starting transfers between devices, body(): lax.all_to_all(state, 'box', split_axis=2, concat_axis=2, tiled=True)  7.44 us
  transfers between devices with their start and end apart: 5, of which 4 were waited for; matrix products, arithmetic and copies ran while one was open for 13% of the time, Pallas kernels for 0%

commit v1 on v0

v1 whole, which is shorter than its diff:
```python
import jax
import jax.numpy as jnp
from jax import lax
from jax.experimental import pallas as pl
from jax.experimental.pallas import tpu as pltpu
from jax.sharding import PartitionSpec as P

LANES = 128


def levels_kernel(received, tables, picks, order, out, state):
    tiles, rhs, rank, _ = received.shape
    level_count, rows, _ = tables.shape
    table_count = rows // rank
    groups = rank // 8
    boxes = tiles * LANES
    source = lax.broadcasted_iota(jnp.int32, (boxes, 512), 0)

    for level in range(level_count):
        apart = tiles >> (level + 1)
        before = received if level == 0 else state
        for low in range(tiles):
            if low & apart:
                continue
            pair = (low, low + apart)
            joined = jnp.concatenate(
                [jnp.concatenate([before[tile, r] for tile in pair], axis=0) for r in range(rhs)], axis=1
            )
            product = jnp.dot(tables[level], joined, preferred_element_type=jnp.float32)
            product = product.reshape(table_count, groups, 8, rhs * LANES)
            for tile in pair:
                pick = jnp.broadcast_to(picks[level, tile : tile + 1, :], (8, LANES))
                pick = jnp.concatenate([pick] * rhs, axis=1)
                choices = [product[t] for t in range(table_count)]
                bit = 1
                while len(choices) > 1:
                    odd = (pick & bit) != 0
                    choices = [jnp.where(odd, high, low_) for low_, high in zip(choices[::2], choices[1::2])]
                    bit *= 2
                chosen = choices[0].reshape(rank, rhs * LANES).astype(jnp.bfloat16)
                for r in range(rhs):
                    state[tile, r] = chosen[:, r * LANES : (r + 1) * LANES]

    flat = jnp.concatenate([state[tile].reshape(rhs * rank, LANES) for tile in range(tiles)], axis=1)
    for start in range(0, boxes, 512):
        wanted = order[:, start : start + 512]
        hot = jnp.where(source == wanted, 1.0, 0.0).astype(jnp.bfloat16)
        placed = jnp.dot(flat, hot, preferred_element_type=jnp.float32).astype(jnp.bfloat16)
        out[:, :, start : start + 512] = placed.reshape(rhs, rank, 512)


def run_levels(received, tables, picks, order):
    tiles, rhs, rank, _ = received.shape
    return pl.pallas_call(
        levels_kernel,
        out_shape=jax.ShapeDtypeStruct((rhs, rank, tiles * LANES), jnp.bfloat16),
        in_specs=[pl.BlockSpec(memory_space=pltpu.VMEM)] * 4,
        out_specs=pl.BlockSpec(memory_space=pltpu.VMEM),
        scratch_shapes=[pltpu.VMEM((tiles, rhs, rank, LANES), jnp.bfloat16)],
        compiler_params=pltpu.CompilerParams(vmem_limit_bytes=40 * 2**20),
        cost_estimate=pl.CostEstimate(flops=4 * 10**9, bytes_accessed=4 * 2**20, transcendentals=0),
    )(received, tables, picks, order)


def body(coeffs, operators, pattern, owner_order):
    device_count = lax.axis_size("box")
    device_index = lax.axis_index("box")
    rhs, rank, boxes = coeffs.shape
    level_count, table_count = operators.shape[:2]
    piece = boxes // device_count
    tiles = boxes // LANES

    sent = coeffs.reshape(rhs, rank, device_count, piece).transpose(2, 0, 1, 3)
    received = lax.all_to_all(sent, "box", split_axis=0, concat_axis=0, tiled=True)
    received = received.reshape(tiles, device_count // tiles, rhs, rank, piece)
    received = received.transpose(0, 2, 3, 1, 4).reshape(tiles, rhs, rank, LANES)

    picks = pattern.reshape(level_count, device_count, device_count, piece)
    picks = lax.dynamic_index_in_dim(picks, device_index, 2, keepdims=False)
    picks = picks.reshape(level_count, tiles, LANES)
    tables = operators.reshape(level_count, table_count * rank, 2 * rank)
    return run_levels(received, tables, picks, owner_order.reshape(1, boxes))


def solution(mesh):
    return jax.shard_map(
        body,
        mesh=mesh,
        in_specs=(P(None, None, ("groups", "box")), P(), P(None, "groups"), P(("groups", "box"))),
        out_specs=P(None, None, ("groups", "box")),
        check_vma=False,
    )
```

time: 185 us -> 42.7 us (0.23)
  the two profiles are of different devices: /device:TPU:0 before, /device:TPU:11 now
where the time goes in v1:
time: 42.7 us; the launch traced here: 42.4 us
  waiting for transfers between devices  23.6 us (55%)
  Pallas kernels  8.45 us (20%)
  starting transfers between devices  6.61 us (15%)
  local copies, waits for them, and re-layouts  3.67 us (9%)
    all_to_all x1, waiting for transfers between devices, body(): lax.all_to_all(sent, 'box', split_axis=0, concat_axis=0, tiled=True)  23.6 us
    pallas_call x1, Pallas kernels, run_levels(): pl.pallas_call(levels_kernel, out_shape=jax.ShapeDtypeStruct((rhs, rank,...  8.45 us
    all_to_all x1, starting transfers between devices, body(): lax.all_to_all(sent, 'box', split_axis=0, concat_axis=0, tiled=True)  6.61 us
    unnamed x7, local copies, waits for them, and re-layouts  2.37 us
    transpose x1, local copies, waits for them, and re-layouts, body(): sent = coeffs.reshape(rhs, rank, device_count, piece).transpose(2, 0, 1, 3)  1.27 us
  transfers between devices with their start and end apart: 1, of which 1 were waited for; matrix products, arithmetic and copies ran while one was open for 3% of the time, Pallas kernels for 0%

profile of v1, /device:TPU:11, one launch (start us, length us, event | category | flops | bytes accessed | tf_op | source)
XLA Modules:
  0.0 42.4 jit_solution(1447188080919946791)
XLA Ops:
  0.0 0.0 copy-start
  0.0 1.2 %copy-done = bf16[4,64,2048]{2,1,0:T(8,128)(2,1)S(1)} copy-done((bf16[4,64,2048]{2,1,0:T(8,128)(2,1)S(1)}, bf16[4,64,2048]{2,1,0:T(8,128)(2,1)}, u32[]{:S(2)}) %copy-start) | copy-done | bytes 1048600
  1.2 1.3 %bitcast_bitcast_fusion = bf16[16,4,64,128]{3,2,1,0:T(8,128)(2,1)} fusion(bf16[4,64,2048]{2,1,0:T(8,128)(2,1)S(1)} %copy-done), kind=kLoop, calls=%fused_computation | loop fusion | bytes 2097152 | tf_op jit(solution)/shard_map/transpose | solution.py:73
  2.5 6.6 %all-to-all-start = ((bf16[16,4,64,128]{3,2,1,0:T(8,128)(2,1)}), bf16[16,4,64,128]{3,2,1,0:T(8,128)(2,1)S(1)}, u32[]{:S(2)}, u32[]{:S(2)}) async-start(bf16[16,4,64,128]{3,2,1,0:T(8,128)(2,1)} %bitcast_bitcast_fusion), calls=%async_computation | async-start | bytes 2097152 | tf_op jit(solution)/shard_map/all_to_all | solution.py:74
  9.1 0.0 copy-start.1
  9.1 1.1 %copy.10 = s32[1,4,256,128]{3,2,1,0:T(8,128)S(1)} copy(s32[1,4,256,128]{3,1,2,0:T(4,128)} %bitcast.19) | data formatting | bytes 1048576
  10.3 0.0 copy-start.2
  10.3 23.6 %all-to-all-done.received = bf16[16,4,64,128]{3,2,1,0:T(8,128)(2,1)S(1)} async-done(((bf16[16,4,64,128]{3,2,1,0:T(8,128)(2,1)}), bf16[16,4,64,128]{3,2,1,0:T(8,128)(2,1)S(1)}, u32[]{:S(2)}, u32[]{:S(2)}) %all-to-all-start) | async-done | bytes 1048608 | tf_op jit(solution)/shard_map/all_to_all | solution.py:74
  34.0 0.0 copy-done.1
  34.0 0.0 copy-done.2
  34.0 8.4 %shard_map.46 = bf16[4,64,2048]{2,1,0:T(8,128)(2,1)} custom-call(bf16[16,4,64,128]{3,2,1,0:T(8,128)(2,1)S(1)} %all-to-all-done.received, bf16[4,512,128]{2,1,0:T(8,128)(2,1)S(1)} %bitcast.16, s32[4,16,128]{2,1,0:T(8,128)S(1)} %bitcast.15, s32[1,2048]{1,0:T(1,128)S(1)} %bitcast.17), custom_call_target="tpu_custom_call" | custom-call | flops 4000000000 | bytes 4194304 | tf_op jit(solution)/shard_map/pallas_call | solution.py:54
  (1 shorter events, 0.0 us)
Async XLA Ops:
  0.0 1.2 %copy-start = (bf16[4,64,2048]{2,1,0:T(8,128)(2,1)S(1)}, bf16[4,64,2048]{2,1,0:T(8,128)(2,1)}, u32[]{:S(2)}) copy-start(bf16[4,64,2048]{2,1,0:T(8,128)(2,1)} %param.4) | copy-start | bytes 3145732
  2.5 31.5 %all-to-all-start = ((bf16[16,4,64,128]{3,2,1,0:T(8,128)(2,1)}), bf16[16,4,64,128]{3,2,1,0:T(8,128)(2,1)S(1)}, u32[]{:S(2)}, u32[]{:S(2)}) async-start(bf16[16,4,64,128]{3,2,1,0:T(8,128)(2,1)} %bitcast_bitcast_fusion), calls=%async_computation | async-start | bytes 2097152 | tf_op jit(solution)/shard_map/all_to_all | solution.py:74
  9.1 24.8 %copy-start.1 = (bf16[4,8,64,128]{3,2,1,0:T(8,128)(2,1)S(1)}, bf16[4,8,64,128]{3,2,1,0:T(8,128)(2,1)}, u32[]{:S(2)}) copy-start(bf16[4,8,64,128]{3,2,1,0:T(8,128)(2,1)} %param.5) | copy-start | bytes 1572868
  10.3 23.7 %copy-start.2 = (s32[2048]{0:T(1024)S(1)}, s32[2048]{0:T(1024)}, u32[]{:S(2)}) copy-start(s32[2048]{0:T(1024)} %param.7) | copy-start | bytes 24580

commit v2 on v1

v2 whole, which is shorter than its diff:
```python
import functools

import jax
import jax.numpy as jnp
from jax import lax
from jax.experimental import pallas as pl
from jax.experimental.pallas import tpu as pltpu
from jax.sharding import PartitionSpec as P

LANES = 128
STRIP = 512
LATE = 1
NEAR = 4
PACK_VMEM = 56 * 2**20
VMEM = pl.BlockSpec(memory_space=pltpu.VMEM)
SMEM = pl.BlockSpec(memory_space=pltpu.SMEM)


import functools

import jax
import jax.numpy as jnp
from jax import lax
from jax.experimental import pallas as pl
from jax.experimental.pallas import tpu as pltpu
from jax.sharding import PartitionSpec as P

LANES = 128
EARLY = 2
PACK_VMEM = 56 * 2**20
NEAR = 4
VMEM = pl.BlockSpec(memory_space=pltpu.VMEM)
SMEM = pl.BlockSpec(memory_space=pltpu.SMEM)


def pack_kernel(me, coeffs, most, *refs):
    near, sem = refs[:-1], refs[-1]
    devices, first = most.shape[:2]
    rhs = coeffs.shape[0]
    copies = []
    for j in range(devices):
        copies.append((coeffs.at[0:first, :, j * LANES : (j + 1) * LANES], most.at[j]))
    for d, ref in enumerate(near):
        for s in range(ref.shape[0]):
            tile = me[0] ^ (s * NEAR + d)
            lanes = pl.ds(pl.multiple_of(tile * LANES, LANES), LANES)
            copies.append((coeffs.at[first:rhs, :, lanes], ref.at[s]))
    copies = [pltpu.make_async_copy(a, b, sem.at[n]) for n, (a, b) in enumerate(copies)]
    for copy in copies:
        copy.start()
    for copy in copies:
        copy.wait()


def pack(me, coeffs, late):
    rhs, rank, boxes = coeffs.shape
    devices = boxes // LANES
    shapes = [(devices, rhs - late, rank, LANES)] + [(devices // NEAR, late, rank, LANES)] * NEAR
    return pl.pallas_call(
        pack_kernel,
        out_shape=[jax.ShapeDtypeStruct(s, coeffs.dtype) for s in shapes],
        in_specs=[SMEM, pl.BlockSpec(memory_space=pl.ANY)],
        out_specs=[VMEM] * len(shapes),
        scratch_shapes=[pltpu.SemaphoreType.DMA((2 * devices,))],
        compiler_params=pltpu.CompilerParams(vmem_limit_bytes=PACK_VMEM),
    )(me, coeffs)


def regroup_kernel(*refs):
    count = refs[-1].shape[0]
    before, after = refs[:count], refs[count:]
    for j, ref in enumerate(after):
        for i in range(count):
            ref[i] = before[i][j]


def regroup(before):
    count = before[0].shape[0]
    shape = (len(before), *before[0].shape[1:])
    return pl.pallas_call(
        regroup_kernel,
        out_shape=[jax.ShapeDtypeStruct(shape, before[0].dtype)] * count,
        in_specs=[VMEM] * len(before),
        out_specs=[VMEM] * count,
        compiler_params=pltpu.CompilerParams(vmem_limit_bytes=8 * 2**20),
    )(*before)


def all_levels(source, tables, picks, state, rhs):
    tiles, _, rank, _ = state.shape
    level_count, rows, _ = tables.shape
    table_count = rows // rank
    for level in range(level_count):
        apart = tiles >> (level + 1)
        before = source if level == 0 else lambda tile, r: state[tile, r]
        for low in range(tiles):
            if low & apart:
                continue
            pair = (low, low + apart)
            joined = jnp.concatenate(
                [jnp.concatenate([before(tile, r) for tile in pair], axis=0) for r in range(rhs)], axis=1
            )
            product = jnp.dot(tables[level], joined, preferred_element_type=jnp.float32)
            product = product.reshape(table_count, rank // 8, 8, rhs * LANES)
            for tile in pair:
                pick = jnp.broadcast_to(picks[level, tile : tile + 1, :], (8, LANES))
                pick = jnp.concatenate([pick] * rhs, axis=1)
                choices = [product[t] for t in range(table_count)]
                bit = 1
                while len(choices) > 1:
                    odd = (pick & bit) != 0
                    choices = [jnp.where(odd, b, a) for a, b in zip(choices[::2], choices[1::2])]
                    bit *= 2
                chosen = choices[0].reshape(rank, rhs * LANES).astype(jnp.bfloat16)
                for r in range(rhs):
                    state[tile, r] = chosen[:, r * LANES : (r + 1) * LANES]


def lay_out(states, order, out, placed, sem):
    rows = []
    for state in states:
        tiles, rhs, rank, _ = state.shape
        rows.append(jnp.concatenate([state[tile].reshape(rhs * rank, LANES) for tile in range(tiles)], axis=1))
    flat = jnp.concatenate(rows, axis=0)
    source = lax.broadcasted_iota(jnp.int32, (out.shape[2], STRIP), 0)
    copies = []
    for number, start in enumerate(range(0, out.shape[2], STRIP)):
        columns = slice(start, start + STRIP)
        hot = jnp.where(source == order[:, columns], 1.0, 0.0).astype(jnp.bfloat16)
        strip = jnp.dot(flat, hot, preferred_element_type=jnp.float32)
        placed[:, :, columns] = strip.astype(jnp.bfloat16).reshape(out.shape[0], rank, STRIP)
        copies.append(pltpu.make_async_copy(placed.at[:, :, columns], out.at[:, :, columns], sem.at[number]))
        copies[-1].start()
    for copy in copies:
        copy.wait()


def first_kernel(received, tables, picks, state):
    all_levels(lambda tile, r: received[tile, r], tables, picks, state, received.shape[1])


def run_first(received, tables, picks):
    rhs = received.shape[1]
    return pl.pallas_call(
        first_kernel,
        out_shape=jax.ShapeDtypeStruct(received.shape, jnp.bfloat16),
        in_specs=[VMEM] * 3,
        out_specs=VMEM,
        compiler_params=pltpu.CompilerParams(vmem_limit_bytes=16 * 2**20),
        cost_estimate=pl.CostEstimate(flops=rhs * 10**9, bytes_accessed=rhs * 2**20, transcendentals=0),
    )(received, tables, picks)


def last_kernel(me, tables, picks, order, done, *refs):
    far, (out, state, placed, sem) = refs[:-4], refs[-4:]
    states = [done]
    if far:
        for s, ref in enumerate(far):
            for d in range(NEAR):
                state[me[0] ^ (s * NEAR + d)] = ref[d]
        all_levels(lambda tile, r: state[tile, r], tables, picks, state, state.shape[1])
        states.append(state)
    lay_out(states, order, out, placed, sem)


def run_last(me, tables, picks, order, done, far):
    tiles, first, rank, _ = done.shape
    boxes, late = tiles * LANES, far[0].shape[1] if far else 0
    return pl.pallas_call(
        last_kernel,
        out_shape=jax.ShapeDtypeStruct((first + late, rank, boxes), jnp.bfloat16),
        in_specs=[SMEM] + [VMEM] * (4 + len(far)),
        out_specs=pl.BlockSpec(memory_space=pl.ANY),
        scratch_shapes=[
            pltpu.VMEM((tiles, max(late, 1), rank, LANES), jnp.bfloat16),
            pltpu.VMEM((first + late, rank, boxes), jnp.bfloat16),
            pltpu.SemaphoreType.DMA((boxes // STRIP,)),
        ],
        compiler_params=pltpu.CompilerParams(vmem_limit_bytes=40 * 2**20),
        cost_estimate=pl.CostEstimate(flops=5 * 10**9, bytes_accessed=2 * 2**20, transcendentals=0),
    )(me, tables, picks, order, done, *far)


def across(block, distance):
    count = lax.axis_size("box")
    return lax.ppermute(block, "box", [(i, i ^ distance) for i in range(count)])


def body(coeffs, operators, pattern, owner_order):
    device_count = lax.axis_size("box")
    device_index = lax.axis_index("box")
    rhs, rank, boxes = coeffs.shape
    level_count, table_count = operators.shape[:2]
    piece = boxes // device_count
    tiles = boxes // LANES
    picks = pattern.reshape(level_count, device_count, device_count, piece)
    picks = lax.dynamic_index_in_dim(picks, device_index, 2, keepdims=False)
    picks = picks.reshape(level_count, tiles, LANES)
    tables = operators.reshape(level_count, table_count * rank, 2 * rank)
    me = device_index.reshape(1).astype(jnp.int32)
    order = owner_order.reshape(1, boxes)

    if piece != LANES:
        sent = coeffs.reshape(rhs, rank, device_count, piece).transpose(2, 0, 1, 3)
        received = lax.all_to_all(sent, "box", split_axis=0, concat_axis=0, tiled=True)
        received = received.reshape(tiles, device_count // tiles, rhs, rank, piece)
        received = received.transpose(0, 2, 3, 1, 4).reshape(tiles, rhs, rank, LANES)
        return run_last(me, tables, picks, order, run_first(received, tables, picks), [])

    most, *near = pack(me, coeffs, LATE)
    received = lax.all_to_all(most, "box", split_axis=0, concat_axis=0, tiled=True)
    near = [near[0]] + [across(near[d], d) for d in range(1, NEAR)]
    far = regroup(near)
    far = [far[0]] + [across(far[s], s * NEAR) for s in range(1, len(far))]
    done = run_first(received, tables, picks)
    return run_last(me, tables, picks, order, done, far)


def solution(mesh):
    return jax.shard_map(
        body,
        mesh=mesh,
        in_specs=(P(None, None, ("groups", "box")), P(), P(None, "groups"), P(("groups", "box"))),
        out_specs=P(None, None, ("groups", "box")),
        check_vma=False,
    )
```

time: 42.7 us -> 40.5 us (0.948)
  the two profiles are of different devices: /device:TPU:11 before, /device:TPU:0 now
where the time goes in v2:
time: 40.5 us; the launch traced here: 40.2 us
  starting transfers between devices  14.7 us (36%)
  waiting for transfers between devices  14.6 us (36%)
  Pallas kernels  10.7 us (26%)
    ppermute x6, waiting for transfers between devices, across(): return lax.ppermute(block, 'box', [(i, i ^ distance) for i in range(count)])  11.2 us
    all_to_all x1, starting transfers between devices, body(): lax.all_to_all(most, 'box', split_axis=0, concat_axis=0, tiled=True)  7.53 us
    ppermute x6, starting transfers between devices, across(): return lax.ppermute(block, 'box', [(i, i ^ distance) for i in range(count)])  7.21 us
    pallas_call x1, Pallas kernels, run_last(): pl.pallas_call(last_kernel, out_shape=jax.ShapeDtypeStruct((first + late,...  4.56 us
    pallas_call x1, Pallas kernels, run_first(): pl.pallas_call(first_kernel, out_shape=jax.ShapeDtypeStruct(received.shap...  3.68 us
    all_to_all x1, waiting for transfers between devices, body(): lax.all_to_all(most, 'box', split_axis=0, concat_axis=0, tiled=True)  3.37 us
    pallas_call x1, Pallas kernels, pack(): pl.pallas_call(pack_kernel, out_shape=[jax.ShapeDtypeStruct(s, coeffs.dty...  2.4 us
  transfers between devices with their start and end apart: 7, of which 4 were waited for; matrix products, arithmetic and copies ran while one was open for 0% of the time, Pallas kernels for 9%

profile of v2, /device:TPU:0, one launch (start us, length us, event | category | flops | bytes accessed | tf_op | source)
XLA Modules:
  0.0 40.2 jit_solution(3300974277103044830)
XLA Ops:
  0.0 2.4 %shard_map.46 = (bf16[16,3,64,128]{3,2,1,0:T(8,128)(2,1)}, bf16[4,1,64,128]{3,2,1,0:T(8,128)(2,1)}, bf16[4,1,64,128]{3,2,1,0:T(8,128)(2,1)}, bf16[4,1,64,128]{3,2,1,0:T(8,128)(2,1)}, bf16[4,1,64,128]{3,2,1,0:T(8,128)(2,1)}) custom-call(s32[1]{0:T(128)} %bitcast.me, bf16[4,64,2048]{2,1,0:T(8,128)(2,1)} %coeffs.1), custom_call_target="tpu_custom_call" | custom-call | tf_op jit(solution)/shard_map/pallas_call | solution.py:59
  2.4 0.0 copy-start.6
  2.4 0.0 copy-start.5
  2.4 0.0 copy-start.4
  2.4 0.0 copy-start.3
  2.4 7.5 %all-to-all-start = ((bf16[16,3,64,128]{3,2,1,0:T(8,128)(2,1)}), bf16[16,3,64,128]{3,2,1,0:T(8,128)(2,1)S(1)}, u32[]{:S(2)}, u32[]{:S(2)}) async-start(bf16[16,3,64,128]{3,2,1,0:T(8,128)(2,1)} %get-tuple-element.14), calls=%async_computation | async-start | bytes 1572864 | tf_op jit(solution)/shard_map/all_to_all | solution.py:211
  10.0 0.0 copy-done.6
  10.0 0.5 %collective-permute-start = (bf16[4,1,64,128]{3,2,1,0:T(8,128)(2,1)S(1)}, bf16[4,1,64,128]{3,2,1,0:T(8,128)(2,1)S(1)}, u32[]{:S(2)}, u32[]{:S(2)}) collective-permute-start(bf16[4,1,64,128]{3,2,1,0:T(8,128)(2,1)S(1)} %copy-done.6), channel_id=1, source_target_pairs={{0,1},{1,0},{2,3},{3,2},{4,5},{5,4},{6,7},{7,6},{8,9},{9,8},{10,11... | collective-permute-start | bytes 196616 | tf_op jit(solution)/shard_map/ppermute | solution.py:186
  10.5 0.0 copy-done.5
  10.5 1.7 %collective-permute-start.1 = (bf16[4,1,64,128]{3,2,1,0:T(8,128)(2,1)S(1)}, bf16[4,1,64,128]{3,2,1,0:T(8,128)(2,1)S(1)}, u32[]{:S(2)}, u32[]{:S(2)}) collective-permute-start(bf16[4,1,64,128]{3,2,1,0:T(8,128)(2,1)S(1)} %copy-done.5), channel_id=1, source_target_pairs={{0,2},{1,3},{2,0},{3,1},{4,6},{5,7},{6,4},{7,5},{8,10},{9,11},{10,... | collective-permute-start | bytes 196616 | tf_op jit(solution)/shard_map/ppermute | solution.py:186
  12.1 0.0 copy-done.4
  12.1 0.0 collective-permute-start.2
  12.2 0.0 copy-done.3
  12.2 0.0 copy-start.1
  12.2 0.0 copy-start
  12.3 0.0 collective-permute-done.refs_1_
  12.3 7.8 %collective-permute-done.1.refs_2_ = bf16[4,1,64,128]{3,2,1,0:T(8,128)(2,1)S(1)} collective-permute-done((bf16[4,1,64,128]{3,2,1,0:T(8,128)(2,1)S(1)}, bf16[4,1,64,128]{3,2,1,0:T(8,128)(2,1)S(1)}, u32[]{:S(2)}, u32[]{:S(2)}) %collective-permute-start.1) | collective-permute-done | bytes 65568 | tf_op jit(solution)/shard_map/ppermute | solution.py:186
  20.0 0.6 %collective-permute-done.2.refs_3_ = bf16[4,1,64,128]{3,2,1,0:T(8,128)(2,1)S(1)} collective-permute-done((bf16[4,1,64,128]{3,2,1,0:T(8,128)(2,1)S(1)}, bf16[4,1,64,128]{3,2,1,0:T(8,128)(2,1)S(1)}, u32[]{:S(2)}, u32[]{:S(2)}) %collective-permute-start.2) | collective-permute-done | bytes 65568 | tf_op jit(solution)/shard_map/ppermute | solution.py:186
  20.6 0.0 copy-done
  20.7 1.2 %collective-permute-start.3 = (bf16[4,1,64,128]{3,2,1,0:T(8,128)(2,1)S(1)}, bf16[4,1,64,128]{3,2,1,0:T(8,128)(2,1)S(1)}, u32[]{:S(2)}, u32[]{:S(2)}) collective-permute-start(bf16[4,1,64,128]{3,2,1,0:T(8,128)(2,1)S(1)} %get-tuple-element.20), channel_id=1, source_target_pairs={{0,4},{1,5},{2,6},{3,7},{4,0},{5,1},{6,2},{7,3},{8,12},{9,13},{10,... | collective-permute-start | bytes 196616 | tf_op jit(solution)/shard_map/ppermute | solution.py:186
  21.9 3.8 %collective-permute-start.4 = (bf16[4,1,64,128]{3,2,1,0:T(8,128)(2,1)S(1)}, bf16[4,1,64,128]{3,2,1,0:T(8,128)(2,1)S(1)}, u32[]{:S(2)}, u32[]{:S(2)}) collective-permute-start(bf16[4,1,64,128]{3,2,1,0:T(8,128)(2,1)S(1)} %get-tuple-element.21), channel_id=1, source_target_pairs={{0,8},{1,9},{2,10},{3,11},{4,12},{5,13},{6,14},{7,15},{8,0},{9,1},... | collective-permute-start | bytes 196616 | tf_op jit(solution)/shard_map/ppermute | solution.py:186
  25.7 0.0 collective-permute-start.5
  25.7 3.4 %all-to-all-done.received = bf16[16,3,64,128]{3,2,1,0:T(8,128)(2,1)S(1)} async-done(((bf16[16,3,64,128]{3,2,1,0:T(8,128)(2,1)}), bf16[16,3,64,128]{3,2,1,0:T(8,128)(2,1)S(1)}, u32[]{:S(2)}, u32[]{:S(2)}) %all-to-all-start) | async-done | bytes 786464 | tf_op jit(solution)/shard_map/all_to_all | solution.py:211
  29.1 0.0 copy-done.1
  29.1 0.0 copy-start.2
  29.1 3.7 %shard_map.47.done = bf16[16,3,64,128]{3,2,1,0:T(8,128)(2,1)S(1)} custom-call(bf16[16,3,64,128]{3,2,1,0:T(8,128)(2,1)S(1)} %all-to-all-done.received, bf16[4,512,128]{2,1,0:T(8,128)(2,1)S(1)} %bitcast.11, s32[4,16,128]{2,1,0:T(8,128)S(1)} %bitcast.9), custom_call_target="tpu_custom_call" | custom-call | flops 3000000000 | bytes 3145728 | tf_op jit(solution)/shard_map/pallas_call | solution.py:144
  32.8 0.0 collective-permute-done.3.refs_1_
  32.8 2.8 %collective-permute-done.4.refs_2_ = bf16[4,1,64,128]{3,2,1,0:T(8,128)(2,1)S(1)} collective-permute-done((bf16[4,1,64,128]{3,2,1,0:T(8,128)(2,1)S(1)}, bf16[4,1,64,128]{3,2,1,0:T(8,128)(2,1)S(1)}, u32[]{:S(2)}, u32[]{:S(2)}) %collective-permute-start.4) | collective-permute-done | bytes 65568 | tf_op jit(solution)/shard_map/ppermute | solution.py:186
  35.6 0.0 collective-permute-done.5.refs_3_
  35.6 0.0 copy-done.2
  35.6 4.6 %shard_map.49 = bf16[4,64,2048]{2,1,0:T(8,128)(2,1)} custom-call(s32[1]{0:T(128)} %bitcast.me, bf16[4,512,128]{2,1,0:T(8,128)(2,1)S(1)} %bitcast.12, s32[4,16,128]{2,1,0:T(8,128)S(1)} %bitcast.10, s32[1,2048]{1,0:T(1,128)S(1)} %bitcast.13, bf16[16,3,64,128]{3,2,1,0:T(8,128)(2,1)S(1)} %shard_map.47.done, ...), custom_call_target="tpu_custom_call" | custom-call | flops 5000000000 | bytes 2097152 | tf_op jit(solution)/shard_map/pallas_call | solution.py:169
  (3 shorter events, 0.1 us)
Async XLA Ops:
  2.4 7.6 %copy-start.6 = (bf16[4,1,64,128]{3,2,1,0:T(8,128)(2,1)S(1)}, bf16[4,1,64,128]{3,2,1,0:T(8,128)(2,1)}, u32[]{:S(2)}) copy-start(bf16[4,1,64,128]{3,2,1,0:T(8,128)(2,1)} %get-tuple-element.16) | copy-start | bytes 196612
  2.4 8.1 %copy-start.5 = (bf16[4,1,64,128]{3,2,1,0:T(8,128)(2,1)S(1)}, bf16[4,1,64,128]{3,2,1,0:T(8,128)(2,1)}, u32[]{:S(2)}) copy-start(bf16[4,1,64,128]{3,2,1,0:T(8,128)(2,1)} %get-tuple-element.17) | copy-start | bytes 196612
  2.4 9.7 %copy-start.4 = (bf16[4,1,64,128]{3,2,1,0:T(8,128)(2,1)S(1)}, bf16[4,1,64,128]{3,2,1,0:T(8,128)(2,1)}, u32[]{:S(2)}) copy-start(bf16[4,1,64,128]{3,2,1,0:T(8,128)(2,1)} %get-tuple-element.18) | copy-start | bytes 196612
  2.4 9.7 %copy-start.3 = (s32[4,32768]{1,0:T(4,128)S(1)}, s32[4,32768]{1,0:T(4,128)}, u32[]{:S(2)}) copy-start(s32[4,32768]{1,0:T(4,128)} %param.6) | copy-start | bytes 1572868
  2.4 26.6 %all-to-all-start = ((bf16[16,3,64,128]{3,2,1,0:T(8,128)(2,1)}), bf16[16,3,64,128]{3,2,1,0:T(8,128)(2,1)S(1)}, u32[]{:S(2)}, u32[]{:S(2)}) async-start(bf16[16,3,64,128]{3,2,1,0:T(8,128)(2,1)} %get-tuple-element.14), calls=%async_computation | async-start | bytes 1572864 | tf_op jit(solution)/shard_map/all_to_all | solution.py:211
  10.0 2.3 %collective-permute-start = (bf16[4,1,64,128]{3,2,1,0:T(8,128)(2,1)S(1)}, bf16[4,1,64,128]{3,2,1,0:T(8,128)(2,1)S(1)}, u32[]{:S(2)}, u32[]{:S(2)}) collective-permute-start(bf16[4,1,64,128]{3,2,1,0:T(8,128)(2,1)S(1)} %copy-done.6), channel_id=1, source_target_pairs={{0,1},{1,0},{2,3},{3,2},{4,5},{5,4},{6,7},{7,6},{8,9},{9,8},{10,11... | collective-permute-start | bytes 196616 | tf_op jit(solution)/shard_map/ppermute | solution.py:186
  10.5 9.6 %collective-permute-start.1 = (bf16[4,1,64,128]{3,2,1,0:T(8,128)(2,1)S(1)}, bf16[4,1,64,128]{3,2,1,0:T(8,128)(2,1)S(1)}, u32[]{:S(2)}, u32[]{:S(2)}) collective-permute-start(bf16[4,1,64,128]{3,2,1,0:T(8,128)(2,1)S(1)} %copy-done.5), channel_id=1, source_target_pairs={{0,2},{1,3},{2,0},{3,1},{4,6},{5,7},{6,4},{7,5},{8,10},{9,11},{10,... | collective-permute-start | bytes 196616 | tf_op jit(solution)/shard_map/ppermute | solution.py:186
  12.1 8.5 %collective-permute-start.2 = (bf16[4,1,64,128]{3,2,1,0:T(8,128)(2,1)S(1)}, bf16[4,1,64,128]{3,2,1,0:T(8,128)(2,1)S(1)}, u32[]{:S(2)}, u32[]{:S(2)}) collective-permute-start(bf16[4,1,64,128]{3,2,1,0:T(8,128)(2,1)S(1)} %copy-done.4), channel_id=1, source_target_pairs={{0,3},{1,2},{2,1},{3,0},{4,7},{5,6},{6,5},{7,4},{8,11},{9,10},{10,... | collective-permute-start | bytes 196616 | tf_op jit(solution)/shard_map/ppermute | solution.py:186
  12.2 16.9 %copy-start.1 = (bf16[4,8,64,128]{3,2,1,0:T(8,128)(2,1)S(1)}, bf16[4,8,64,128]{3,2,1,0:T(8,128)(2,1)}, u32[]{:S(2)}) copy-start(bf16[4,8,64,128]{3,2,1,0:T(8,128)(2,1)} %param.5) | copy-start | bytes 1572868
  12.2 8.4 %copy-start = (bf16[4,1,64,128]{3,2,1,0:T(8,128)(2,1)S(1)}, bf16[4,1,64,128]{3,2,1,0:T(8,128)(2,1)}, u32[]{:S(2)}) copy-start(bf16[4,1,64,128]{3,2,1,0:T(8,128)(2,1)} %get-tuple-element.15.refs_0_) | copy-start | bytes 196612
  20.7 12.1 %collective-permute-start.3 = (bf16[4,1,64,128]{3,2,1,0:T(8,128)(2,1)S(1)}, bf16[4,1,64,128]{3,2,1,0:T(8,128)(2,1)S(1)}, u32[]{:S(2)}, u32[]{:S(2)}) collective-permute-start(bf16[4,1,64,128]{3,2,1,0:T(8,128)(2,1)S(1)} %get-tuple-element.20), channel_id=1, source_target_pairs={{0,4},{1,5},{2,6},{3,7},{4,0},{5,1},{6,2},{7,3},{8,12},{9,13},{10,... | collective-permute-start | bytes 196616 | tf_op jit(solution)/shard_map/ppermute | solution.py:186
  21.9 13.7 %collective-permute-start.4 = (bf16[4,1,64,128]{3,2,1,0:T(8,128)(2,1)S(1)}, bf16[4,1,64,128]{3,2,1,0:T(8,128)(2,1)S(1)}, u32[]{:S(2)}, u32[]{:S(2)}) collective-permute-start(bf16[4,1,64,128]{3,2,1,0:T(8,128)(2,1)S(1)} %get-tuple-element.21), channel_id=1, source_target_pairs={{0,8},{1,9},{2,10},{3,11},{4,12},{5,13},{6,14},{7,15},{8,0},{9,1},... | collective-permute-start | bytes 196616 | tf_op jit(solution)/shard_map/ppermute | solution.py:186
  25.7 9.9 %collective-permute-start.5 = (bf16[4,1,64,128]{3,2,1,0:T(8,128)(2,1)S(1)}, bf16[4,1,64,128]{3,2,1,0:T(8,128)(2,1)S(1)}, u32[]{:S(2)}, u32[]{:S(2)}) collective-permute-start(bf16[4,1,64,128]{3,2,1,0:T(8,128)(2,1)S(1)} %get-tuple-element.22), channel_id=1, source_target_pairs={{0,12},{1,13},{2,14},{3,15},{4,8},{5,9},{6,10},{7,11},{8,4},{9,5},... | collective-permute-start | bytes 196616 | tf_op jit(solution)/shard_map/ppermute | solution.py:186
  29.1 6.5 %copy-start.2 = (s32[2048]{0:T(1024)S(1)}, s32[2048]{0:T(1024)}, u32[]{:S(2)}) copy-start(s32[2048]{0:T(1024)} %param.7) | copy-start | bytes 24580

commit v3 on v1

v3 whole, which is shorter than its diff:
```python
import functools

import jax
import jax.numpy as jnp
from jax import lax
from jax.experimental import pallas as pl
from jax.experimental.pallas import tpu as pltpu
from jax.sharding import PartitionSpec as P

LANES = 128
STRIP = 512
EARLY = 2
NEAR = 4
PACK_VMEM = 52 * 2**20
EARLY_COST = 16
FIRST_COST = 2
FIRST_VMEM = 24 * 2**20
LAST_VMEM = 24 * 2**20
VMEM = pl.BlockSpec(memory_space=pltpu.VMEM)
SMEM = pl.BlockSpec(memory_space=pltpu.SMEM)


import functools

import jax
import jax.numpy as jnp
from jax import lax
from jax.experimental import pallas as pl
from jax.experimental.pallas import tpu as pltpu
from jax.sharding import PartitionSpec as P

LANES = 128
EARLY = 2
PACK_VMEM = 52 * 2**20
FIRST_COST = 2
NEAR = 4
VMEM = pl.BlockSpec(memory_space=pltpu.VMEM)
SMEM = pl.BlockSpec(memory_space=pltpu.SMEM)


def pack_kernel(early, me, coeffs, operators, pattern, tables, picks, *refs):
    refs, sem = refs[:-1], refs[-1]
    near, far = refs[:NEAR], refs[NEAR:]
    rhs, _, boxes = coeffs.shape
    copies = [(operators, tables)]
    for tile in range(picks.shape[0]):
        lanes = pl.ds(pl.multiple_of(tile * boxes + me[0] * LANES, LANES), LANES)
        copies.append((pattern.at[:, lanes], picks.at[tile]))
    for s in range(len(far)):
        for d in range(NEAR):
            tile = me[0] ^ (s * NEAR + d)
            lanes = pl.ds(pl.multiple_of(tile * LANES, LANES), LANES)
            copies.append((coeffs.at[0:early, :, lanes], far[s].at[d]))
            tile = s * NEAR + ((me[0] % NEAR) ^ d)
            lanes = pl.ds(pl.multiple_of(tile * LANES, LANES), LANES)
            copies.append((coeffs.at[early:rhs, :, lanes], near[d].at[s]))
    copies = [pltpu.make_async_copy(a, b, sem.at[n]) for n, (a, b) in enumerate(copies)]
    for copy in copies:
        copy.start()
    for copy in copies:
        copy.wait()


def pack(me, coeffs, operators, pattern, early):
    rhs, rank, boxes = coeffs.shape
    tiles = boxes // LANES
    planes = tiles // NEAR
    shapes = [(planes, rhs - early, rank, LANES)] * NEAR + [(NEAR, early, rank, LANES)] * planes
    packed = pl.pallas_call(
        functools.partial(pack_kernel, early),
        out_shape=[
            jax.ShapeDtypeStruct(operators.shape, operators.dtype),
            jax.ShapeDtypeStruct((tiles, pattern.shape[0], LANES), pattern.dtype),
        ]
        + [jax.ShapeDtypeStruct(s, coeffs.dtype) for s in shapes],
        in_specs=[SMEM] + [pl.BlockSpec(memory_space=pl.ANY)] * 3,
        out_specs=[VMEM] * (2 + len(shapes)),
        scratch_shapes=[pltpu.SemaphoreType.DMA((1 + 3 * tiles,))],
        compiler_params=pltpu.CompilerParams(vmem_limit_bytes=PACK_VMEM),
    )(me, coeffs, operators, pattern)
    return packed[:2], packed[2 : 2 + NEAR], packed[2 + NEAR :]


def late_kernel(*refs):
    near, late = refs[:-1], refs[-1]
    for d, ref in enumerate(near):
        for z in range(late.shape[0]):
            late[z, d] = ref[z]


def late_blocks(near):
    planes = near[0].shape[0]
    return pl.pallas_call(
        late_kernel,
        out_shape=jax.ShapeDtypeStruct((planes, len(near), *near[0].shape[1:]), near[0].dtype),
        in_specs=[VMEM] * len(near),
        out_specs=VMEM,
        compiler_params=pltpu.CompilerParams(vmem_limit_bytes=8 * 2**20),
    )(*near)


def early_kernel(*refs):
    far, early = refs[:-NEAR], refs[-NEAR:]
    for s, ref in enumerate(far):
        for d in range(NEAR):
            early[d][s] = ref[d]


def early_blocks(far):
    return pl.pallas_call(
        early_kernel,
        out_shape=[jax.ShapeDtypeStruct((len(far), *far[0].shape[1:]), far[0].dtype)] * NEAR,
        in_specs=[VMEM] * len(far),
        out_specs=[VMEM] * NEAR,
        compiler_params=pltpu.CompilerParams(vmem_limit_bytes=8 * 2**20),
        cost_estimate=pl.CostEstimate(flops=EARLY_COST * 10**9, bytes_accessed=2**10, transcendentals=0),
    )(*far)


def all_levels(source, tables, picks, state, rhs):
    tiles, _, rank, _ = state.shape
    level_count, rows, _ = tables.shape
    table_count = rows // rank
    for level in range(level_count):
        apart = tiles >> (level + 1)
        before = source if level == 0 else lambda tile, r: state[tile, r]
        for low in range(tiles):
            if low & apart:
                continue
            pair = (low, low + apart)
            joined = jnp.concatenate(
                [jnp.concatenate([before(tile, r) for tile in pair], axis=0) for r in range(rhs)], axis=1
            )
            product = jnp.dot(tables[level], joined, preferred_element_type=jnp.float32)
            product = product.reshape(table_count, rank // 8, 8, rhs * LANES)
            for tile in pair:
                pick = jnp.broadcast_to(picks[tile, level : level + 1, :], (8, LANES))
                pick = jnp.concatenate([pick] * rhs, axis=1)
                choices = [product[t] for t in range(table_count)]
                bit = 1
                while len(choices) > 1:
                    odd = (pick & bit) != 0
                    choices = [jnp.where(odd, b, a) for a, b in zip(choices[::2], choices[1::2])]
                    bit *= 2
                chosen = choices[0].reshape(rank, rhs * LANES).astype(jnp.bfloat16)
                for r in range(rhs):
                    state[tile, r] = chosen[:, r * LANES : (r + 1) * LANES]


def flat_rows(state):
    tiles, rhs, rank, _ = state.shape
    return jnp.concatenate([state[tile].reshape(rhs * rank, LANES) for tile in range(tiles)], axis=1)


def ones_at(order, start):
    source = lax.broadcasted_iota(jnp.int32, (order.shape[1], STRIP), 0)
    return jnp.where(source == order[:, start : start + STRIP], 1.0, 0.0).astype(jnp.bfloat16)


def put(flat, hot, placed, start):
    strip = jnp.dot(flat, hot, preferred_element_type=jnp.float32).astype(jnp.bfloat16)
    placed[:, :, start : start + STRIP] = strip.reshape(*placed.shape[:2], STRIP)


def whole_kernel(received, tables, picks, order, out, state):
    all_levels(lambda tile, r: received[tile, r], tables, picks, state, received.shape[1])
    flat = flat_rows(state)
    for start in range(0, out.shape[2], STRIP):
        put(flat, ones_at(order, start), out, start)


def run_whole(received, tables, picks, order):
    tiles, rhs, rank, _ = received.shape
    return pl.pallas_call(
        whole_kernel,
        out_shape=jax.ShapeDtypeStruct((rhs, rank, tiles * LANES), jnp.bfloat16),
        in_specs=[VMEM] * 4,
        out_specs=VMEM,
        scratch_shapes=[pltpu.VMEM(received.shape, jnp.bfloat16)],
        compiler_params=pltpu.CompilerParams(vmem_limit_bytes=40 * 2**20),
    )(received, tables, picks, order)


def first_kernel(me, tables, picks, *refs):
    near, state = refs[:-1], refs[-1]
    for d, ref in enumerate(near):
        for s in range(ref.shape[0]):
            state[me[0] ^ (s * NEAR + d)] = ref[s]
    all_levels(lambda tile, r: state[tile, r], tables, picks, state, state.shape[1])


def run_first(me, tables, picks, near):
    planes, rhs, rank, _ = near[0].shape
    return pl.pallas_call(
        first_kernel,
        out_shape=jax.ShapeDtypeStruct((planes * len(near), rhs, rank, LANES), jnp.bfloat16),
        in_specs=[SMEM] + [VMEM] * (2 + len(near)),
        out_specs=VMEM,
        compiler_params=pltpu.CompilerParams(vmem_limit_bytes=FIRST_VMEM),
        cost_estimate=pl.CostEstimate(flops=FIRST_COST * 10**9, bytes_accessed=2**10, transcendentals=0),
    )(me, tables, picks, *near)


def last_kernel(me, tables, picks, order, done, late, out, state, placed, sem):
    for z in range(late.shape[0]):
        for d in range(NEAR):
            state[z * NEAR + ((me[0] % NEAR) ^ d)] = late[z, d]
    all_levels(lambda tile, r: state[tile, r], tables, picks, state, state.shape[1])
    flat = jnp.concatenate([flat_rows(done), flat_rows(state)], axis=0)
    copies = []
    for start in range(0, out.shape[2], STRIP):
        columns = slice(start, start + STRIP)
        put(flat, ones_at(order, start), placed, start)
        copies.append(pltpu.make_async_copy(placed.at[:, :, columns], out.at[:, :, columns], sem.at[start // STRIP]))
        copies[-1].start()
    for copy in copies:
        copy.wait()


def run_last(me, tables, picks, order, done, late):
    tiles, early, rank, _ = done.shape
    boxes, more = tiles * LANES, late.shape[2]
    return pl.pallas_call(
        last_kernel,
        out_shape=jax.ShapeDtypeStruct((early + more, rank, boxes), jnp.bfloat16),
        in_specs=[SMEM] + [VMEM] * 5,
        out_specs=pl.BlockSpec(memory_space=pl.ANY),
        scratch_shapes=[
            pltpu.VMEM((tiles, more, rank, LANES), jnp.bfloat16),
            pltpu.VMEM((early + more, rank, boxes), jnp.bfloat16),
            pltpu.SemaphoreType.DMA((boxes // STRIP,)),
        ],
        compiler_params=pltpu.CompilerParams(vmem_limit_bytes=LAST_VMEM),
        cost_estimate=pl.CostEstimate(flops=5 * 10**9, bytes_accessed=2 * 2**20, transcendentals=0),
    )(me, tables, picks, order, done, late)


def across(block, distance):
    count = lax.axis_size("box")
    return lax.ppermute(block, "box", [(i, i ^ distance) for i in range(count)])


def body(coeffs, operators, pattern, owner_order):
    device_count = lax.axis_size("box")
    device_index = lax.axis_index("box")
    rhs, rank, boxes = coeffs.shape
    level_count, table_count = operators.shape[:2]
    piece = boxes // device_count
    tiles = boxes // LANES
    me = device_index.reshape(1).astype(jnp.int32)
    order = owner_order.reshape(1, boxes)
    tables = operators.reshape(level_count, table_count * rank, 2 * rank)

    if piece != LANES:
        picks = pattern.reshape(level_count, device_count, device_count, piece)
        picks = lax.dynamic_index_in_dim(picks, device_index, 2, keepdims=False)
        picks = picks.reshape(level_count, tiles, LANES).transpose(1, 0, 2)
        sent = coeffs.reshape(rhs, rank, device_count, piece).transpose(2, 0, 1, 3)
        received = lax.all_to_all(sent, "box", split_axis=0, concat_axis=0, tiled=True)
        received = received.reshape(tiles, device_count // tiles, rhs, rank, piece)
        received = received.transpose(0, 2, 3, 1, 4).reshape(tiles, rhs, rank, LANES)
        return run_whole(received, tables, picks, order)

    (tables, picks), near, far = pack(me, coeffs, tables, pattern, EARLY)
    far = [far[0]] + [across(far[s], s * NEAR) for s in range(1, len(far))]
    near = [near[0]] + [across(near[d], d) for d in range(1, NEAR)]
    columns = [[z * NEAR + d for z in range(len(far))] for d in range(NEAR)]
    late = lax.all_to_all(late_blocks(near), "box", 0, 0, tiled=True, axis_index_groups=columns)
    early = early_blocks(far)
    early = [early[0]] + [across(early[d], d) for d in range(1, NEAR)]
    done = run_first(me, tables, picks, early)
    return run_last(me, tables, picks, order, done, late)


def solution(mesh):
    return jax.shard_map(
        body,
        mesh=mesh,
        in_specs=(P(None, None, ("groups", "box")), P(), P(None, "groups"), P(("groups", "box"))),
        out_specs=P(None, None, ("groups", "box")),
        check_vma=False,
    )
```

time: 42.7 us -> 38.8 us (0.909)
  the two profiles are of different devices: /device:TPU:11 before, /device:TPU:0 now
where the time goes in v3:
time: 38.8 us; the launch traced here: 38.6 us
  starting transfers between devices  14.4 us (37%)
  waiting for transfers between devices  13 us (34%)
  Pallas kernels  11.1 us (29%)
    ppermute x9, waiting for transfers between devices, across(): return lax.ppermute(block, 'box', [(i, i ^ distance) for i in range(count)])  11 us
    ppermute x9, starting transfers between devices, across(): return lax.ppermute(block, 'box', [(i, i ^ distance) for i in range(count)])  9.5 us
    pallas_call x1, Pallas kernels, run_last(): pl.pallas_call(last_kernel, out_shape=jax.ShapeDtypeStruct((early + more,...  5.71 us
    all_to_all x1, starting transfers between devices, body(): lax.all_to_all(late_blocks(near), 'box', 0, 0, tiled=True, axis_index_gro...  4.92 us
    pallas_call x1, Pallas kernels, run_first(): pl.pallas_call(first_kernel, out_shape=jax.ShapeDtypeStruct((planes * len...  2.74 us
    all_to_all x1, waiting for transfers between devices, body(): lax.all_to_all(late_blocks(near), 'box', 0, 0, tiled=True, axis_index_gro...  2.01 us
    pallas_call x1, Pallas kernels, pack(): pl.pallas_call(functools.partial(pack_kernel, early), out_shape=[jax.Shap...  1.82 us
    pallas_call x1, Pallas kernels, late_blocks(): pl.pallas_call(late_kernel, out_shape=jax.ShapeDtypeStruct((planes, len(n...  0.83 us
  transfers between devices with their start and end apart: 10, of which 5 were waited for; matrix products, arithmetic and copies ran while one was open for 0% of the time, Pallas kernels for 9%

profile of v3, /device:TPU:0, one launch (start us, length us, event | category | flops | bytes accessed | tf_op | source)
XLA Modules:
  0.0 38.6 jit_solution(7748367321125165218)
XLA Ops:
  0.0 1.8 %shard_map.46 = (bf16[4,512,128]{2,1,0:T(8,128)(2,1)S(1)}, s32[16,4,128]{2,1,0:T(4,128)S(1)}, bf16[4,2,64,128]{3,2,1,0:T(8,128)(2,1)S(1)}, bf16[4,2,64,128]{3,2,...) custom-call(s32[1]{0:T(128)} %bitcast.me, ...), custom_call_target="tpu_custom_call" | custom-call | tf_op jit(solution)/shard_map/pallas_call | solution.py:69
  1.8 0.5 %collective-permute-start.6 = (bf16[4,2,64,128]{3,2,1,0:T(8,128)(2,1)S(1)}, bf16[4,2,64,128]{3,2,1,0:T(8,128)(2,1)S(1)}, u32[]{:S(2)}, u32[]{:S(2)}) collective-permute-start(bf16[4,2,64,128]{3,2,1,0:T(8,128)(2,1)S(1)} %get-tuple-element.30), channel_id=1, source_target_pairs={{0,1},{1,0},{2,3},{3,2},{4,5},{5,4},{6,7},{7,6},{8,9},{9,8},{10,11... | collective-permute-start | bytes 393224 | tf_op jit(solution)/shard_map/ppermute | solution.py:240
  2.4 2.6 %collective-permute-start.7 = (bf16[4,2,64,128]{3,2,1,0:T(8,128)(2,1)S(1)}, bf16[4,2,64,128]{3,2,1,0:T(8,128)(2,1)S(1)}, u32[]{:S(2)}, u32[]{:S(2)}) collective-permute-start(bf16[4,2,64,128]{3,2,1,0:T(8,128)(2,1)S(1)} %get-tuple-element.31), channel_id=1, source_target_pairs={{0,2},{1,3},{2,0},{3,1},{4,6},{5,7},{6,4},{7,5},{8,10},{9,11},{10,... | collective-permute-start | bytes 393224 | tf_op jit(solution)/shard_map/ppermute | solution.py:240
  4.9 0.1 collective-permute-start.8
  5.0 1.8 %collective-permute-start = (bf16[4,2,64,128]{3,2,1,0:T(8,128)(2,1)S(1)}, bf16[4,2,64,128]{3,2,1,0:T(8,128)(2,1)S(1)}, u32[]{:S(2)}, u32[]{:S(2)}) collective-permute-start(bf16[4,2,64,128]{3,2,1,0:T(8,128)(2,1)S(1)} %get-tuple-element.22), channel_id=1, source_target_pairs={{0,4},{1,5},{2,6},{3,7},{4,0},{5,1},{6,2},{7,3},{8,12},{9,13},{10,... | collective-permute-start | bytes 393224 | tf_op jit(solution)/shard_map/ppermute | solution.py:240
  6.8 2.6 %collective-permute-start.1 = (bf16[4,2,64,128]{3,2,1,0:T(8,128)(2,1)S(1)}, bf16[4,2,64,128]{3,2,1,0:T(8,128)(2,1)S(1)}, u32[]{:S(2)}, u32[]{:S(2)}) collective-permute-start(bf16[4,2,64,128]{3,2,1,0:T(8,128)(2,1)S(1)} %get-tuple-element.23), channel_id=1, source_target_pairs={{0,8},{1,9},{2,10},{3,11},{4,12},{5,13},{6,14},{7,15},{8,0},{9,1},... | collective-permute-start | bytes 393224 | tf_op jit(solution)/shard_map/ppermute | solution.py:240
  9.4 0.0 collective-permute-done.6.refs_1_
  9.4 0.0 collective-permute-start.2
  9.4 0.0 collective-permute-done.7.refs_2_
  9.4 2.2 %collective-permute-done.8.refs_3_ = bf16[4,2,64,128]{3,2,1,0:T(8,128)(2,1)S(1)} collective-permute-done((bf16[4,2,64,128]{3,2,1,0:T(8,128)(2,1)S(1)}, bf16[4,2,64,128]{3,2,1,0:T(8,128)(2,1)S(1)}, u32[]{:S(2)}, u32[]{:S(2)}) %collective-permute-start.8) | collective-permute-done | bytes 131104 | tf_op jit(solution)/shard_map/ppermute | solution.py:240
  11.6 0.8 %shard_map.49 = bf16[4,4,2,64,128]{4,3,2,1,0:T(8,128)(2,1)} custom-call(bf16[4,2,64,128]{3,2,1,0:T(8,128)(2,1)S(1)} %get-tuple-element.29.refs_0_, bf16[4,2,64,128]{3,2,1,0:T(8,128)(2,1)S(1)} %collective-permute-done.6.refs_1_, bf16[4,2,64,128]{3,2,1,0:T(8,128)(2,1)S(1)} %collective-permute-done.7.refs_2_, ...), custom_call_target="tpu_custom_call" | custom-call | tf_op jit(solution)/shard_map/pallas_call | solution.py:93
  12.4 4.9 %all-to-all-start = ((bf16[4,4,2,64,128]{4,3,2,1,0:T(8,128)(2,1)}), bf16[4,4,2,64,128]{4,3,2,1,0:T(8,128)(2,1)S(1)}, u32[]{:S(2)}, u32[]{:S(2)}) async-start(bf16[4,4,2,64,128]{4,3,2,1,0:T(8,128)(2,1)} %shard_map.49), calls=%async_computation | async-start | bytes 1048576 | tf_op jit(solution)/shard_map/all_to_all | solution.py:268
  17.3 0.0 collective-permute-done.refs_1_
  17.3 2.4 %collective-permute-done.1.refs_2_ = bf16[4,2,64,128]{3,2,1,0:T(8,128)(2,1)S(1)} collective-permute-done((bf16[4,2,64,128]{3,2,1,0:T(8,128)(2,1)S(1)}, bf16[4,2,64,128]{3,2,1,0:T(8,128)(2,1)S(1)}, u32[]{:S(2)}, u32[]{:S(2)}) %collective-permute-start.1) | collective-permute-done | bytes 131104 | tf_op jit(solution)/shard_map/ppermute | solution.py:240
  19.7 0.0 collective-permute-done.2.refs_3_
  19.8 0.1 collective-permute-start.3
  19.8 1.6 %collective-permute-start.4 = (bf16[4,2,64,128]{3,2,1,0:T(8,128)(2,1)S(1)}, bf16[4,2,64,128]{3,2,1,0:T(8,128)(2,1)S(1)}, u32[]{:S(2)}, u32[]{:S(2)}) collective-permute-start(bf16[4,2,64,128]{3,2,1,0:T(8,128)(2,1)S(1)} %get-tuple-element.27), channel_id=1, source_target_pairs={{0,2},{1,3},{2,0},{3,1},{4,6},{5,7},{6,4},{7,5},{8,10},{9,11},{10,... | collective-permute-start | bytes 393224 | tf_op jit(solution)/shard_map/ppermute | solution.py:240
  21.4 0.3 collective-permute-start.5
  21.7 0.0 collective-permute-done.3.refs_1_
  21.7 4.5 %collective-permute-done.4.refs_2_ = bf16[4,2,64,128]{3,2,1,0:T(8,128)(2,1)S(1)} collective-permute-done((bf16[4,2,64,128]{3,2,1,0:T(8,128)(2,1)S(1)}, bf16[4,2,64,128]{3,2,1,0:T(8,128)(2,1)S(1)}, u32[]{:S(2)}, u32[]{:S(2)}) %collective-permute-start.4) | collective-permute-done | bytes 131104 | tf_op jit(solution)/shard_map/ppermute | solution.py:240
  26.2 1.9 %collective-permute-done.5.refs_3_ = bf16[4,2,64,128]{3,2,1,0:T(8,128)(2,1)S(1)} collective-permute-done((bf16[4,2,64,128]{3,2,1,0:T(8,128)(2,1)S(1)}, bf16[4,2,64,128]{3,2,1,0:T(8,128)(2,1)S(1)}, u32[]{:S(2)}, u32[]{:S(2)}) %collective-permute-start.5) | collective-permute-done | bytes 131104 | tf_op jit(solution)/shard_map/ppermute | solution.py:240
  28.1 0.0 copy-start
  28.1 2.7 %shard_map.48.done = bf16[16,2,64,128]{3,2,1,0:T(8,128)(2,1)S(1)} custom-call(s32[1]{0:T(128)} %bitcast.me, bf16[4,512,128]{2,1,0:T(8,128)(2,1)S(1)} %get-tuple-element.19.tables, s32[16,4,128]{2,1,0:T(4,128)S(1)} %get-tuple-element.20.picks, bf16[4,2,64,128]{3,2,1,0:T(8,128)(2,1)S(1)} %get-tuple-element.25.refs_0_, ...), custom_call_target="tpu_custom_call" | custom-call | flops 2000000000 | bytes 1024 | tf_op jit(solution)/shard_map/pallas_call | solution.py:194
  30.9 2.0 %all-to-all-done.late = bf16[4,4,2,64,128]{4,3,2,1,0:T(8,128)(2,1)S(1)} async-done(((bf16[4,4,2,64,128]{4,3,2,1,0:T(8,128)(2,1)}), bf16[4,4,2,64,128]{4,3,2,1,0:T(8,128)(2,1)S(1)}, u32[]{:S(2)}, u32[]{:S(2)}) %all-to-all-start) | async-done | bytes 524320 | tf_op jit(solution)/shard_map/all_to_all | solution.py:268
  32.9 0.0 copy-done
  32.9 5.7 %shard_map.50 = bf16[4,64,2048]{2,1,0:T(8,128)(2,1)} custom-call(s32[1]{0:T(128)} %bitcast.me, bf16[4,512,128]{2,1,0:T(8,128)(2,1)S(1)} %get-tuple-element.19.tables, s32[16,4,128]{2,1,0:T(4,128)S(1)} %get-tuple-element.20.picks, s32[1,2048]{1,0:T(1,128)S(1)} %bitcast.3, bf16[16,2,64,128]{3,2,1,0:T(8,128)(2,1)S(1)} %shard_map.48.done, ...), custom_call_target="tpu_custom_call" | custom-call | flops 5000000000 | bytes 2097152 | tf_op jit(solution)/shard_map/pallas_call | solution.py:223
  (1 shorter events, 0.0 us)
Async XLA Ops:
  1.8 7.6 %collective-permute-start.6 = (bf16[4,2,64,128]{3,2,1,0:T(8,128)(2,1)S(1)}, bf16[4,2,64,128]{3,2,1,0:T(8,128)(2,1)S(1)}, u32[]{:S(2)}, u32[]{:S(2)}) collective-permute-start(bf16[4,2,64,128]{3,2,1,0:T(8,128)(2,1)S(1)} %get-tuple-element.30), channel_id=1, source_target_pairs={{0,1},{1,0},{2,3},{3,2},{4,5},{5,4},{6,7},{7,6},{8,9},{9,8},{10,11... | collective-permute-start | bytes 393224 | tf_op jit(solution)/shard_map/ppermute | solution.py:240
  2.4 7.1 %collective-permute-start.7 = (bf16[4,2,64,128]{3,2,1,0:T(8,128)(2,1)S(1)}, bf16[4,2,64,128]{3,2,1,0:T(8,128)(2,1)S(1)}, u32[]{:S(2)}, u32[]{:S(2)}) collective-permute-start(bf16[4,2,64,128]{3,2,1,0:T(8,128)(2,1)S(1)} %get-tuple-element.31), channel_id=1, source_target_pairs={{0,2},{1,3},{2,0},{3,1},{4,6},{5,7},{6,4},{7,5},{8,10},{9,11},{10,... | collective-permute-start | bytes 393224 | tf_op jit(solution)/shard_map/ppermute | solution.py:240
  4.9 6.6 %collective-permute-start.8 = (bf16[4,2,64,128]{3,2,1,0:T(8,128)(2,1)S(1)}, bf16[4,2,64,128]{3,2,1,0:T(8,128)(2,1)S(1)}, u32[]{:S(2)}, u32[]{:S(2)}) collective-permute-start(bf16[4,2,64,128]{3,2,1,0:T(8,128)(2,1)S(1)} %get-tuple-element.32), channel_id=1, source_target_pairs={{0,3},{1,2},{2,1},{3,0},{4,7},{5,6},{6,5},{7,4},{8,11},{9,10},{10,... | collective-permute-start | bytes 393224 | tf_op jit(solution)/shard_map/ppermute | solution.py:240
  5.0 12.3 %collective-permute-start = (bf16[4,2,64,128]{3,2,1,0:T(8,128)(2,1)S(1)}, bf16[4,2,64,128]{3,2,1,0:T(8,128)(2,1)S(1)}, u32[]{:S(2)}, u32[]{:S(2)}) collective-permute-start(bf16[4,2,64,128]{3,2,1,0:T(8,128)(2,1)S(1)} %get-tuple-element.22), channel_id=1, source_target_pairs={{0,4},{1,5},{2,6},{3,7},{4,0},{5,1},{6,2},{7,3},{8,12},{9,13},{10,... | collective-permute-start | bytes 393224 | tf_op jit(solution)/shard_map/ppermute | solution.py:240
  6.8 12.9 %collective-permute-start.1 = (bf16[4,2,64,128]{3,2,1,0:T(8,128)(2,1)S(1)}, bf16[4,2,64,128]{3,2,1,0:T(8,128)(2,1)S(1)}, u32[]{:S(2)}, u32[]{:S(2)}) collective-permute-start(bf16[4,2,64,128]{3,2,1,0:T(8,128)(2,1)S(1)} %get-tuple-element.23), channel_id=1, source_target_pairs={{0,8},{1,9},{2,10},{3,11},{4,12},{5,13},{6,14},{7,15},{8,0},{9,1},... | collective-permute-start | bytes 393224 | tf_op jit(solution)/shard_map/ppermute | solution.py:240
  9.4 10.3 %collective-permute-start.2 = (bf16[4,2,64,128]{3,2,1,0:T(8,128)(2,1)S(1)}, bf16[4,2,64,128]{3,2,1,0:T(8,128)(2,1)S(1)}, u32[]{:S(2)}, u32[]{:S(2)}) collective-permute-start(bf16[4,2,64,128]{3,2,1,0:T(8,128)(2,1)S(1)} %get-tuple-element.24), channel_id=1, source_target_pairs={{0,12},{1,13},{2,14},{3,15},{4,8},{5,9},{6,10},{7,11},{8,4},{9,5},... | collective-permute-start | bytes 393224 | tf_op jit(solution)/shard_map/ppermute | solution.py:240
  12.4 20.5 %all-to-all-start = ((bf16[4,4,2,64,128]{4,3,2,1,0:T(8,128)(2,1)}), bf16[4,4,2,64,128]{4,3,2,1,0:T(8,128)(2,1)S(1)}, u32[]{:S(2)}, u32[]{:S(2)}) async-start(bf16[4,4,2,64,128]{4,3,2,1,0:T(8,128)(2,1)} %shard_map.49), calls=%async_computation | async-start | bytes 1048576 | tf_op jit(solution)/shard_map/all_to_all | solution.py:268
  19.8 1.9 %collective-permute-start.3 = (bf16[4,2,64,128]{3,2,1,0:T(8,128)(2,1)S(1)}, bf16[4,2,64,128]{3,2,1,0:T(8,128)(2,1)S(1)}, u32[]{:S(2)}, u32[]{:S(2)}) collective-permute-start(bf16[4,2,64,128]{3,2,1,0:T(8,128)(2,1)S(1)} %get-tuple-element.26), channel_id=1, source_target_pairs={{0,1},{1,0},{2,3},{3,2},{4,5},{5,4},{6,7},{7,6},{8,9},{9,8},{10,11... | collective-permute-start | bytes 393224 | tf_op jit(solution)/shard_map/ppermute | solution.py:240
  19.8 6.4 %collective-permute-start.4 = (bf16[4,2,64,128]{3,2,1,0:T(8,128)(2,1)S(1)}, bf16[4,2,64,128]{3,2,1,0:T(8,128)(2,1)S(1)}, u32[]{:S(2)}, u32[]{:S(2)}) collective-permute-start(bf16[4,2,64,128]{3,2,1,0:T(8,128)(2,1)S(1)} %get-tuple-element.27), channel_id=1, source_target_pairs={{0,2},{1,3},{2,0},{3,1},{4,6},{5,7},{6,4},{7,5},{8,10},{9,11},{10,... | collective-permute-start | bytes 393224 | tf_op jit(solution)/shard_map/ppermute | solution.py:240
  21.4 6.7 %collective-permute-start.5 = (bf16[4,2,64,128]{3,2,1,0:T(8,128)(2,1)S(1)}, bf16[4,2,64,128]{3,2,1,0:T(8,128)(2,1)S(1)}, u32[]{:S(2)}, u32[]{:S(2)}) collective-permute-start(bf16[4,2,64,128]{3,2,1,0:T(8,128)(2,1)S(1)} %get-tuple-element.28), channel_id=1, source_target_pairs={{0,3},{1,2},{2,1},{3,0},{4,7},{5,6},{6,5},{7,4},{8,11},{9,10},{10,... | collective-permute-start | bytes 393224 | tf_op jit(solution)/shard_map/ppermute | solution.py:240
  28.1 4.8 %copy-start = (s32[2048]{0:T(1024)S(1)}, s32[2048]{0:T(1024)}, u32[]{:S(2)}) copy-start(s32[2048]{0:T(1024)} %param.7) | copy-start | bytes 24580

commit v4 on v3

--- a/solution.py
+++ b/solution.py
@@ -20,22 +20,8 @@
 SMEM = pl.BlockSpec(memory_space=pltpu.SMEM)
 
 
-import functools
-
-import jax
-import jax.numpy as jnp
-from jax import lax
-from jax.experimental import pallas as pl
-from jax.experimental.pallas import tpu as pltpu
-from jax.sharding import PartitionSpec as P
-
-LANES = 128
-EARLY = 2
-PACK_VMEM = 52 * 2**20
-FIRST_COST = 2
-NEAR = 4
-VMEM = pl.BlockSpec(memory_space=pltpu.VMEM)
-SMEM = pl.BlockSpec(memory_space=pltpu.SMEM)
+def in_turn(count):
+    return [0] + list(range(max(count // 2, 1), count)) + list(range(1, count // 2))
 
 
 def pack_kernel(early, me, coeffs, operators, pattern, tables, picks, *refs):
@@ -83,7 +69,7 @@
 
 def late_kernel(*refs):
     near, late = refs[:-1], refs[-1]
-    for d, ref in enumerate(near):
+    for d, ref in zip(in_turn(NEAR), near):
         for z in range(late.shape[0]):
             late[z, d] = ref[z]
 
@@ -101,7 +87,7 @@
 
 def early_kernel(*refs):
     far, early = refs[:-NEAR], refs[-NEAR:]
-    for s, ref in enumerate(far):
+    for s, ref in zip(in_turn(len(far)), far):
         for d in range(NEAR):
             early[d][s] = ref[d]
 
@@ -181,45 +167,53 @@
     )(received, tables, picks, order)
 
 
-def first_kernel(me, tables, picks, *refs):
-    near, state = refs[:-1], refs[-1]
-    for d, ref in enumerate(near):
+def first_kernel(me, tables, picks, order, *refs):
+    near, (placed, state) = refs[:-2], refs[-2:]
+    for d, ref in zip(in_turn(NEAR), near):
         for s in range(ref.shape[0]):
             state[me[0] ^ (s * NEAR + d)] = ref[s]
     all_levels(lambda tile, r: state[tile, r], tables, picks, state, state.shape[1])
-
-
-def run_first(me, tables, picks, near):
+    flat = flat_rows(state)
+    for start in range(0, placed.shape[2], STRIP):
+        put(flat, ones_at(order, start), placed, start)
+
+
+def run_first(me, tables, picks, order, near):
     planes, rhs, rank, _ = near[0].shape
+    tiles = planes * len(near)
     return pl.pallas_call(
         first_kernel,
-        out_shape=jax.ShapeDtypeStruct((planes * len(near), rhs, rank, LANES), jnp.bfloat16),
-        in_specs=[SMEM] + [VMEM] * (2 + len(near)),
+        out_shape=jax.ShapeDtypeStruct((rhs, rank, tiles * LANES), jnp.bfloat16),
+        in_specs=[SMEM] + [VMEM] * (3 + len(near)),
         out_specs=VMEM,
+        scratch_shapes=[pltpu.VMEM((tiles, rhs, rank, LANES), jnp.bfloat16)],
         compiler_params=pltpu.CompilerParams(vmem_limit_bytes=FIRST_VMEM),
         cost_estimate=pl.CostEstimate(flops=FIRST_COST * 10**9, bytes_accessed=2**10, transcendentals=0),
-    )(me, tables, picks, *near)
+    )(me, tables, picks, order, *near)
 
 
 def last_kernel(me, tables, picks, order, done, late, out, state, placed, sem):
+    early, rhs = done.shape[0], out.shape[0]
+    copies = [pltpu.make_async_copy(done, out.at[0:early], sem.at[0])]
+    copies[0].start()
     for z in range(late.shape[0]):
         for d in range(NEAR):
             state[z * NEAR + ((me[0] % NEAR) ^ d)] = late[z, d]
     all_levels(lambda tile, r: state[tile, r], tables, picks, state, state.shape[1])
-    flat = jnp.concatenate([flat_rows(done), flat_rows(state)], axis=0)
-    copies = []
-    for start in range(0, out.shape[2], STRIP):
+    flat = flat_rows(state)
+    for number, start in enumerate(range(0, out.shape[2], STRIP)):
         columns = slice(start, start + STRIP)
         put(flat, ones_at(order, start), placed, start)
-        copies.append(pltpu.make_async_copy(placed.at[:, :, columns], out.at[:, :, columns], sem.at[start // STRIP]))
-        copies[-1].start()
+        copy = pltpu.make_async_copy(placed.at[:, :, columns], out.at[early:rhs, :, columns], sem.at[1 + number])
+        copy.start()
+        copies.append(copy)
     for copy in copies:
         copy.wait()
 
 
 def run_last(me, tables, picks, order, done, late):
-    tiles, early, rank, _ = done.shape
-    boxes, more = tiles * LANES, late.shape[2]
+    early, rank, boxes = done.shape
+    tiles, more = boxes // LANES, late.shape[2]
     return pl.pallas_call(
         last_kernel,
         out_shape=jax.ShapeDtypeStruct((early + more, rank, boxes), jnp.bfloat16),
@@ -227,8 +221,8 @@
         out_specs=pl.BlockSpec(memory_space=pl.ANY),
         scratch_shapes=[
             pltpu.VMEM((tiles, more, rank, LANES), jnp.bfloat16),
-            pltpu.VMEM((early + more, rank, boxes), jnp.bfloat16),
-            pltpu.SemaphoreType.DMA((boxes // STRIP,)),
+            pltpu.VMEM((more, rank, boxes), jnp.bfloat16),
+            pltpu.SemaphoreType.DMA((1 + boxes // STRIP,)),
         ],
         compiler_params=pltpu.CompilerParams(vmem_limit_bytes=LAST_VMEM),
         cost_estimate=pl.CostEstimate(flops=5 * 10**9, bytes_accessed=2 * 2**20, transcendentals=0),
@@ -236,6 +230,8 @@
 
 
 def across(block, distance):
+    if distance == 0:
+        return block
     count = lax.axis_size("box")
     return lax.ppermute(block, "box", [(i, i ^ distance) for i in range(count)])
 
@@ -262,13 +258,14 @@
         return run_whole(received, tables, picks, order)
 
     (tables, picks), near, far = pack(me, coeffs, tables, pattern, EARLY)
-    far = [far[0]] + [across(far[s], s * NEAR) for s in range(1, len(far))]
-    near = [near[0]] + [across(near[d], d) for d in range(1, NEAR)]
-    columns = [[z * NEAR + d for z in range(len(far))] for d in range(NEAR)]
+    planes = len(far)
+    far = [across(far[s], s * NEAR) for s in in_turn(planes)]
+    near = [across(near[d], d) for d in in_turn(NEAR)]
+    columns = [[z * NEAR + d for z in range(planes)] for d in range(NEAR)]
     late = lax.all_to_all(late_blocks(near), "box", 0, 0, tiled=True, axis_index_groups=columns)
     early = early_blocks(far)
-    early = [early[0]] + [across(early[d], d) for d in range(1, NEAR)]
-    done = run_first(me, tables, picks, early)
+    early = [across(early[d], d) for d in in_turn(NEAR)]
+    done = run_first(me, tables, picks, order, early)
     return run_last(me, tables, picks, order, done, late)
 
 

time: 38.8 us -> 36.9 us (0.951)
  waiting for transfers between devices: 13 us -> 9.17 us
  starting transfers between devices: 14.4 us -> 15.9 us
  Pallas kernels: 11.1 us -> 11.6 us
    ppermute x9, waiting for transfers between devices: 11 us -> 7.61 us  [across(): return lax.ppermute(block, 'box', [(i, i ^ distance) for i in range(count)])]
    ppermute x9, starting transfers between devices: 9.5 us -> 11.3 us  [across(): return lax.ppermute(block, 'box', [(i, i ^ distance) for i in range(count)])]
    pallas_call x1, Pallas kernels: 2.74 us -> 4.07 us  [run_first(): pl.pallas_call(first_kernel, out_shape=jax.ShapeDtypeStruct((rhs, rank, t...]
    pallas_call x1, Pallas kernels: 5.71 us -> 4.79 us  [run_last(): pl.pallas_call(last_kernel, out_shape=jax.ShapeDtypeStruct((early + more,...]
    all_to_all x1, waiting for transfers between devices: 2.01 us -> 1.57 us  [body(): lax.all_to_all(late_blocks(near), 'box', 0, 0, tiled=True, axis_index_gro...]
  transfers between devices with their start and end apart: 10 -> 10, of which waited for: 5 -> 5; matrix products, arithmetic and copies ran while one was open for 0% -> 0% of each run, Pallas kernels for 9% -> 13%
where the time goes in v4:
time: 36.9 us; the launch traced here: 36.7 us
  starting transfers between devices  15.9 us (43%)
  Pallas kernels  11.6 us (31%)
  waiting for transfers between devices  9.17 us (25%)
    ppermute x9, starting transfers between devices, across(): return lax.ppermute(block, 'box', [(i, i ^ distance) for i in range(count)])  11.3 us
    ppermute x9, waiting for transfers between devices, across(): return lax.ppermute(block, 'box', [(i, i ^ distance) for i in range(count)])  7.61 us
    pallas_call x1, Pallas kernels, run_last(): pl.pallas_call(last_kernel, out_shape=jax.ShapeDtypeStruct((early + more,...  4.79 us
    all_to_all x1, starting transfers between devices, body(): lax.all_to_all(late_blocks(near), 'box', 0, 0, tiled=True, axis_index_gro...  4.62 us
    pallas_call x1, Pallas kernels, run_first(): pl.pallas_call(first_kernel, out_shape=jax.ShapeDtypeStruct((rhs, rank, t...  4.07 us
    pallas_call x1, Pallas kernels, pack(): pl.pallas_call(functools.partial(pack_kernel, early), out_shape=[jax.Shap...  1.82 us
    all_to_all x1, waiting for transfers between devices, body(): lax.all_to_all(late_blocks(near), 'box', 0, 0, tiled=True, axis_index_gro...  1.57 us
    pallas_call x1, Pallas kernels, late_blocks(): pl.pallas_call(late_kernel, out_shape=jax.ShapeDtypeStruct((planes, len(n...  0.83 us
  transfers between devices with their start and end apart: 10, of which 5 were waited for; matrix products, arithmetic and copies ran while one was open for 0% of the time, Pallas kernels for 13%

profile of v4, /device:TPU:0, one launch (start us, length us, event | category | flops | bytes accessed | tf_op | source)
XLA Modules:
  0.0 36.7 jit_solution(6014381336015274739)
XLA Ops:
  0.0 1.8 %shard_map.46 = (bf16[4,512,128]{2,1,0:T(8,128)(2,1)S(1)}, s32[16,4,128]{2,1,0:T(4,128)S(1)}, bf16[4,2,64,128]{3,2,1,0:T(8,128)(2,1)S(1)}, bf16[4,2,64,128]{3,2,...) custom-call(s32[1]{0:T(128)} %bitcast.me, ...), custom_call_target="tpu_custom_call" | custom-call | tf_op jit(solution)/shard_map/pallas_call | solution.py:55
  1.8 3.0 %collective-permute-start.6 = (bf16[4,2,64,128]{3,2,1,0:T(8,128)(2,1)S(1)}, bf16[4,2,64,128]{3,2,1,0:T(8,128)(2,1)S(1)}, u32[]{:S(2)}, u32[]{:S(2)}) collective-permute-start(bf16[4,2,64,128]{3,2,1,0:T(8,128)(2,1)S(1)} %get-tuple-element.30), channel_id=1, source_target_pairs={{0,2},{1,3},{2,0},{3,1},{4,6},{5,7},{6,4},{7,5},{8,10},{9,11},{10,... | collective-permute-start | bytes 393224 | tf_op jit(solution)/shard_map/ppermute | solution.py:236
  4.9 0.0 collective-permute-start.7
  4.9 0.2 collective-permute-start.8
  5.1 3.0 %collective-permute-start = (bf16[4,2,64,128]{3,2,1,0:T(8,128)(2,1)S(1)}, bf16[4,2,64,128]{3,2,1,0:T(8,128)(2,1)S(1)}, u32[]{:S(2)}, u32[]{:S(2)}) collective-permute-start(bf16[4,2,64,128]{3,2,1,0:T(8,128)(2,1)S(1)} %get-tuple-element.22), channel_id=1, source_target_pairs={{0,8},{1,9},{2,10},{3,11},{4,12},{5,13},{6,14},{7,15},{8,0},{9,1},... | collective-permute-start | bytes 393224 | tf_op jit(solution)/shard_map/ppermute | solution.py:236
  8.1 1.3 %collective-permute-start.1 = (bf16[4,2,64,128]{3,2,1,0:T(8,128)(2,1)S(1)}, bf16[4,2,64,128]{3,2,1,0:T(8,128)(2,1)S(1)}, u32[]{:S(2)}, u32[]{:S(2)}) collective-permute-start(bf16[4,2,64,128]{3,2,1,0:T(8,128)(2,1)S(1)} %get-tuple-element.23), channel_id=1, source_target_pairs={{0,12},{1,13},{2,14},{3,15},{4,8},{5,9},{6,10},{7,11},{8,4},{9,5},... | collective-permute-start | bytes 393224 | tf_op jit(solution)/shard_map/ppermute | solution.py:236
  9.4 0.0 collective-permute-done.6.refs_1_
  9.4 1.5 %collective-permute-start.2 = (bf16[4,2,64,128]{3,2,1,0:T(8,128)(2,1)S(1)}, bf16[4,2,64,128]{3,2,1,0:T(8,128)(2,1)S(1)}, u32[]{:S(2)}, u32[]{:S(2)}) collective-permute-start(bf16[4,2,64,128]{3,2,1,0:T(8,128)(2,1)S(1)} %get-tuple-element.24), channel_id=1, source_target_pairs={{0,4},{1,5},{2,6},{3,7},{4,0},{5,1},{6,2},{7,3},{8,12},{9,13},{10,... | collective-permute-start | bytes 393224 | tf_op jit(solution)/shard_map/ppermute | solution.py:236
  10.9 0.0 collective-permute-done.7.refs_2_
  10.9 0.0 collective-permute-done.8.refs_3_
  10.9 0.8 %shard_map.49 = bf16[4,4,2,64,128]{4,3,2,1,0:T(8,128)(2,1)} custom-call(bf16[4,2,64,128]{3,2,1,0:T(8,128)(2,1)S(1)} %get-tuple-element.29.refs_0_, bf16[4,2,64,128]{3,2,1,0:T(8,128)(2,1)S(1)} %collective-permute-done.6.refs_1_, bf16[4,2,64,128]{3,2,1,0:T(8,128)(2,1)S(1)} %collective-permute-done.7.refs_2_, ...), custom_call_target="tpu_custom_call" | custom-call | tf_op jit(solution)/shard_map/pallas_call | solution.py:79
  11.7 4.6 %all-to-all-start = ((bf16[4,4,2,64,128]{4,3,2,1,0:T(8,128)(2,1)}), bf16[4,4,2,64,128]{4,3,2,1,0:T(8,128)(2,1)S(1)}, u32[]{:S(2)}, u32[]{:S(2)}) async-start(bf16[4,4,2,64,128]{4,3,2,1,0:T(8,128)(2,1)} %shard_map.49), calls=%async_computation | async-start | bytes 1048576 | tf_op jit(solution)/shard_map/all_to_all | solution.py:265
  16.4 1.7 %collective-permute-done.refs_1_ = bf16[4,2,64,128]{3,2,1,0:T(8,128)(2,1)S(1)} collective-permute-done((bf16[4,2,64,128]{3,2,1,0:T(8,128)(2,1)S(1)}, bf16[4,2,64,128]{3,2,1,0:T(8,128)(2,1)S(1)}, u32[]{:S(2)}, u32[]{:S(2)}) %collective-permute-start) | collective-permute-done | bytes 131104 | tf_op jit(solution)/shard_map/ppermute | solution.py:236
  18.0 0.0 collective-permute-done.1.refs_2_
  18.0 0.7 %collective-permute-done.2.refs_3_ = bf16[4,2,64,128]{3,2,1,0:T(8,128)(2,1)S(1)} collective-permute-done((bf16[4,2,64,128]{3,2,1,0:T(8,128)(2,1)S(1)}, bf16[4,2,64,128]{3,2,1,0:T(8,128)(2,1)S(1)}, u32[]{:S(2)}, u32[]{:S(2)}) %collective-permute-start.2) | collective-permute-done | bytes 131104 | tf_op jit(solution)/shard_map/ppermute | solution.py:236
  18.8 0.0 copy-start
  18.8 1.6 %collective-permute-start.3 = (bf16[4,2,64,128]{3,2,1,0:T(8,128)(2,1)S(1)}, bf16[4,2,64,128]{3,2,1,0:T(8,128)(2,1)S(1)}, u32[]{:S(2)}, u32[]{:S(2)}) collective-permute-start(bf16[4,2,64,128]{3,2,1,0:T(8,128)(2,1)S(1)} %get-tuple-element.26), channel_id=1, source_target_pairs={{0,2},{1,3},{2,0},{3,1},{4,6},{5,7},{6,4},{7,5},{8,10},{9,11},{10,... | collective-permute-start | bytes 393224 | tf_op jit(solution)/shard_map/ppermute | solution.py:236
  20.4 0.0 collective-permute-start.4
  20.4 0.6 %collective-permute-start.5 = (bf16[4,2,64,128]{3,2,1,0:T(8,128)(2,1)S(1)}, bf16[4,2,64,128]{3,2,1,0:T(8,128)(2,1)S(1)}, u32[]{:S(2)}, u32[]{:S(2)}) collective-permute-start(bf16[4,2,64,128]{3,2,1,0:T(8,128)(2,1)S(1)} %get-tuple-element.28), channel_id=1, source_target_pairs={{0,1},{1,0},{2,3},{3,2},{4,5},{5,4},{6,7},{7,6},{8,9},{9,8},{10,11... | collective-permute-start | bytes 393224 | tf_op jit(solution)/shard_map/ppermute | solution.py:236
  21.0 3.2 %collective-permute-done.3.refs_1_ = bf16[4,2,64,128]{3,2,1,0:T(8,128)(2,1)S(1)} collective-permute-done((bf16[4,2,64,128]{3,2,1,0:T(8,128)(2,1)S(1)}, bf16[4,2,64,128]{3,2,1,0:T(8,128)(2,1)S(1)}, u32[]{:S(2)}, u32[]{:S(2)}) %collective-permute-start.3) | collective-permute-done | bytes 131104 | tf_op jit(solution)/shard_map/ppermute | solution.py:236
  24.2 2.0 %collective-permute-done.4.refs_2_ = bf16[4,2,64,128]{3,2,1,0:T(8,128)(2,1)S(1)} collective-permute-done((bf16[4,2,64,128]{3,2,1,0:T(8,128)(2,1)S(1)}, bf16[4,2,64,128]{3,2,1,0:T(8,128)(2,1)S(1)}, u32[]{:S(2)}, u32[]{:S(2)}) %collective-permute-start.4) | collective-permute-done | bytes 131104 | tf_op jit(solution)/shard_map/ppermute | solution.py:236
  26.2 0.0 collective-permute-done.5.refs_3_
  26.2 0.0 copy-done
  26.2 4.1 %shard_map.48.done = bf16[2,64,2048]{2,1,0:T(8,128)(2,1)S(1)} custom-call(s32[1]{0:T(128)} %bitcast.me, bf16[4,512,128]{2,1,0:T(8,128)(2,1)S(1)} %get-tuple-element.19.tables, s32[16,4,128]{2,1,0:T(4,128)S(1)} %get-tuple-element.20.picks, s32[1,2048]{1,0:T(1,128)S(1)} %bitcast.3, bf16[4,2,64,128]{3,2,1,0:T(8,128)(2,1)S(1)} %get-tuple-element.25.refs_0_, ...), custom_call_target="tpu_custom_call" | custom-call | flops 2000000000 | bytes 1024 | tf_op jit(solution)/shard_map/pallas_call | solution.py:184
  30.3 1.6 %all-to-all-done.late = bf16[4,4,2,64,128]{4,3,2,1,0:T(8,128)(2,1)S(1)} async-done(((bf16[4,4,2,64,128]{4,3,2,1,0:T(8,128)(2,1)}), bf16[4,4,2,64,128]{4,3,2,1,0:T(8,128)(2,1)S(1)}, u32[]{:S(2)}, u32[]{:S(2)}) %all-to-all-start) | async-done | bytes 524320 | tf_op jit(solution)/shard_map/all_to_all | solution.py:265
  31.9 4.8 %shard_map.50 = bf16[4,64,2048]{2,1,0:T(8,128)(2,1)} custom-call(s32[1]{0:T(128)} %bitcast.me, bf16[4,512,128]{2,1,0:T(8,128)(2,1)S(1)} %get-tuple-element.19.tables, s32[16,4,128]{2,1,0:T(4,128)S(1)} %get-tuple-element.20.picks, s32[1,2048]{1,0:T(1,128)S(1)} %bitcast.4, bf16[2,64,2048]{2,1,0:T(8,128)(2,1)S(1)} %shard_map.48.done, ...), custom_call_target="tpu_custom_call" | custom-call | flops 5000000000 | bytes 2097152 | tf_op jit(solution)/shard_map/pallas_call | solution.py:217
  (1 shorter events, 0.0 us)
Async XLA Ops:
  1.8 7.6 %collective-permute-start.6 = (bf16[4,2,64,128]{3,2,1,0:T(8,128)(2,1)S(1)}, bf16[4,2,64,128]{3,2,1,0:T(8,128)(2,1)S(1)}, u32[]{:S(2)}, u32[]{:S(2)}) collective-permute-start(bf16[4,2,64,128]{3,2,1,0:T(8,128)(2,1)S(1)} %get-tuple-element.30), channel_id=1, source_target_pairs={{0,2},{1,3},{2,0},{3,1},{4,6},{5,7},{6,4},{7,5},{8,10},{9,11},{10,... | collective-permute-start | bytes 393224 | tf_op jit(solution)/shard_map/ppermute | solution.py:236
  4.9 6.0 %collective-permute-start.7 = (bf16[4,2,64,128]{3,2,1,0:T(8,128)(2,1)S(1)}, bf16[4,2,64,128]{3,2,1,0:T(8,128)(2,1)S(1)}, u32[]{:S(2)}, u32[]{:S(2)}) collective-permute-start(bf16[4,2,64,128]{3,2,1,0:T(8,128)(2,1)S(1)} %get-tuple-element.31), channel_id=1, source_target_pairs={{0,3},{1,2},{2,1},{3,0},{4,7},{5,6},{6,5},{7,4},{8,11},{9,10},{10,... | collective-permute-start | bytes 393224 | tf_op jit(solution)/shard_map/ppermute | solution.py:236
  4.9 6.0 %collective-permute-start.8 = (bf16[4,2,64,128]{3,2,1,0:T(8,128)(2,1)S(1)}, bf16[4,2,64,128]{3,2,1,0:T(8,128)(2,1)S(1)}, u32[]{:S(2)}, u32[]{:S(2)}) collective-permute-start(bf16[4,2,64,128]{3,2,1,0:T(8,128)(2,1)S(1)} %get-tuple-element.32), channel_id=1, source_target_pairs={{0,1},{1,0},{2,3},{3,2},{4,5},{5,4},{6,7},{7,6},{8,9},{9,8},{10,11... | collective-permute-start | bytes 393224 | tf_op jit(solution)/shard_map/ppermute | solution.py:236
  5.1 13.0 %collective-permute-start = (bf16[4,2,64,128]{3,2,1,0:T(8,128)(2,1)S(1)}, bf16[4,2,64,128]{3,2,1,0:T(8,128)(2,1)S(1)}, u32[]{:S(2)}, u32[]{:S(2)}) collective-permute-start(bf16[4,2,64,128]{3,2,1,0:T(8,128)(2,1)S(1)} %get-tuple-element.22), channel_id=1, source_target_pairs={{0,8},{1,9},{2,10},{3,11},{4,12},{5,13},{6,14},{7,15},{8,0},{9,1},... | collective-permute-start | bytes 393224 | tf_op jit(solution)/shard_map/ppermute | solution.py:236
  8.1 10.0 %collective-permute-start.1 = (bf16[4,2,64,128]{3,2,1,0:T(8,128)(2,1)S(1)}, bf16[4,2,64,128]{3,2,1,0:T(8,128)(2,1)S(1)}, u32[]{:S(2)}, u32[]{:S(2)}) collective-permute-start(bf16[4,2,64,128]{3,2,1,0:T(8,128)(2,1)S(1)} %get-tuple-element.23), channel_id=1, source_target_pairs={{0,12},{1,13},{2,14},{3,15},{4,8},{5,9},{6,10},{7,11},{8,4},{9,5},... | collective-permute-start | bytes 393224 | tf_op jit(solution)/shard_map/ppermute | solution.py:236
  9.4 9.3 %collective-permute-start.2 = (bf16[4,2,64,128]{3,2,1,0:T(8,128)(2,1)S(1)}, bf16[4,2,64,128]{3,2,1,0:T(8,128)(2,1)S(1)}, u32[]{:S(2)}, u32[]{:S(2)}) collective-permute-start(bf16[4,2,64,128]{3,2,1,0:T(8,128)(2,1)S(1)} %get-tuple-element.24), channel_id=1, source_target_pairs={{0,4},{1,5},{2,6},{3,7},{4,0},{5,1},{6,2},{7,3},{8,12},{9,13},{10,... | collective-permute-start | bytes 393224 | tf_op jit(solution)/shard_map/ppermute | solution.py:236
  11.7 20.1 %all-to-all-start = ((bf16[4,4,2,64,128]{4,3,2,1,0:T(8,128)(2,1)}), bf16[4,4,2,64,128]{4,3,2,1,0:T(8,128)(2,1)S(1)}, u32[]{:S(2)}, u32[]{:S(2)}) async-start(bf16[4,4,2,64,128]{4,3,2,1,0:T(8,128)(2,1)} %shard_map.49), calls=%async_computation | async-start | bytes 1048576 | tf_op jit(solution)/shard_map/all_to_all | solution.py:265
  18.8 7.5 %copy-start = (s32[2048]{0:T(1024)S(1)}, s32[2048]{0:T(1024)}, u32[]{:S(2)}) copy-start(s32[2048]{0:T(1024)} %param.7) | copy-start | bytes 24580
  18.8 5.4 %collective-permute-start.3 = (bf16[4,2,64,128]{3,2,1,0:T(8,128)(2,1)S(1)}, bf16[4,2,64,128]{3,2,1,0:T(8,128)(2,1)S(1)}, u32[]{:S(2)}, u32[]{:S(2)}) collective-permute-start(bf16[4,2,64,128]{3,2,1,0:T(8,128)(2,1)S(1)} %get-tuple-element.26), channel_id=1, source_target_pairs={{0,2},{1,3},{2,0},{3,1},{4,6},{5,7},{6,4},{7,5},{8,10},{9,11},{10,... | collective-permute-start | bytes 393224 | tf_op jit(solution)/shard_map/ppermute | solution.py:236
  20.4 5.8 %collective-permute-start.4 = (bf16[4,2,64,128]{3,2,1,0:T(8,128)(2,1)S(1)}, bf16[4,2,64,128]{3,2,1,0:T(8,128)(2,1)S(1)}, u32[]{:S(2)}, u32[]{:S(2)}) collective-permute-start(bf16[4,2,64,128]{3,2,1,0:T(8,128)(2,1)S(1)} %get-tuple-element.27), channel_id=1, source_target_pairs={{0,3},{1,2},{2,1},{3,0},{4,7},{5,6},{6,5},{7,4},{8,11},{9,10},{10,... | collective-permute-start | bytes 393224 | tf_op jit(solution)/shard_map/ppermute | solution.py:236
  20.4 5.8 %collective-permute-start.5 = (bf16[4,2,64,128]{3,2,1,0:T(8,128)(2,1)S(1)}, bf16[4,2,64,128]{3,2,1,0:T(8,128)(2,1)S(1)}, u32[]{:S(2)}, u32[]{:S(2)}) collective-permute-start(bf16[4,2,64,128]{3,2,1,0:T(8,128)(2,1)S(1)} %get-tuple-element.28), channel_id=1, source_target_pairs={{0,1},{1,0},{2,3},{3,2},{4,5},{5,4},{6,7},{7,6},{8,9},{9,8},{10,11... | collective-permute-start | bytes 393224 | tf_op jit(solution)/shard_map/ppermute | solution.py:236

commit v5 on v4

--- a/solution.py
+++ b/solution.py
@@ -14,6 +14,7 @@
 PACK_VMEM = 52 * 2**20
 EARLY_COST = 16
 FIRST_COST = 2
+FETCH_COST = 1
 FIRST_VMEM = 24 * 2**20
 LAST_VMEM = 24 * 2**20
 VMEM = pl.BlockSpec(memory_space=pltpu.VMEM)
@@ -24,14 +25,11 @@
     return [0] + list(range(max(count // 2, 1), count)) + list(range(1, count // 2))
 
 
-def pack_kernel(early, me, coeffs, operators, pattern, tables, picks, *refs):
+def pack_kernel(early, me, coeffs, *refs):
     refs, sem = refs[:-1], refs[-1]
     near, far = refs[:NEAR], refs[NEAR:]
-    rhs, _, boxes = coeffs.shape
-    copies = [(operators, tables)]
-    for tile in range(picks.shape[0]):
-        lanes = pl.ds(pl.multiple_of(tile * boxes + me[0] * LANES, LANES), LANES)
-        copies.append((pattern.at[:, lanes], picks.at[tile]))
+    rhs = coeffs.shape[0]
+    copies = []
     for s in range(len(far)):
         for d in range(NEAR):
             tile = me[0] ^ (s * NEAR + d)
@@ -47,24 +45,48 @@
         copy.wait()
 
 
-def pack(me, coeffs, operators, pattern, early):
+def pack(me, coeffs, early):
     rhs, rank, boxes = coeffs.shape
     tiles = boxes // LANES
     planes = tiles // NEAR
     shapes = [(planes, rhs - early, rank, LANES)] * NEAR + [(NEAR, early, rank, LANES)] * planes
     packed = pl.pallas_call(
         functools.partial(pack_kernel, early),
+        out_shape=[jax.ShapeDtypeStruct(s, coeffs.dtype) for s in shapes],
+        in_specs=[SMEM, pl.BlockSpec(memory_space=pl.ANY)],
+        out_specs=[VMEM] * len(shapes),
+        scratch_shapes=[pltpu.SemaphoreType.DMA((2 * tiles,))],
+        compiler_params=pltpu.CompilerParams(vmem_limit_bytes=PACK_VMEM),
+    )(me, coeffs)
+    return packed[:NEAR], packed[NEAR:]
+
+
+def fetch_kernel(me, operators, pattern, tables, picks, sem):
+    boxes = pattern.shape[1] // picks.shape[0]
+    copies = [(operators, tables)]
+    for tile in range(picks.shape[0]):
+        lanes = pl.ds(pl.multiple_of(tile * boxes + me[0] * LANES, LANES), LANES)
+        copies.append((pattern.at[:, lanes], picks.at[tile]))
+    copies = [pltpu.make_async_copy(a, b, sem.at[n]) for n, (a, b) in enumerate(copies)]
+    for copy in copies:
+        copy.start()
+    for copy in copies:
+        copy.wait()
+
+
+def fetch(me, operators, pattern, tiles):
+    return pl.pallas_call(
+        fetch_kernel,
         out_shape=[
             jax.ShapeDtypeStruct(operators.shape, operators.dtype),
             jax.ShapeDtypeStruct((tiles, pattern.shape[0], LANES), pattern.dtype),
-        ]
-        + [jax.ShapeDtypeStruct(s, coeffs.dtype) for s in shapes],
-        in_specs=[SMEM] + [pl.BlockSpec(memory_space=pl.ANY)] * 3,
-        out_specs=[VMEM] * (2 + len(shapes)),
-        scratch_shapes=[pltpu.SemaphoreType.DMA((1 + 3 * tiles,))],
+        ],
+        in_specs=[SMEM] + [pl.BlockSpec(memory_space=pl.ANY)] * 2,
+        out_specs=[VMEM] * 2,
+        scratch_shapes=[pltpu.SemaphoreType.DMA((1 + tiles,))],
         compiler_params=pltpu.CompilerParams(vmem_limit_bytes=PACK_VMEM),
-    )(me, coeffs, operators, pattern)
-    return packed[:2], packed[2 : 2 + NEAR], packed[2 + NEAR :]
+        cost_estimate=pl.CostEstimate(flops=FETCH_COST * 10**9, bytes_accessed=2**10, transcendentals=0),
+    )(me, operators, pattern)
 
 
 def late_kernel(*refs):
@@ -257,7 +279,8 @@
         received = received.transpose(0, 2, 3, 1, 4).reshape(tiles, rhs, rank, LANES)
         return run_whole(received, tables, picks, order)
 
-    (tables, picks), near, far = pack(me, coeffs, tables, pattern, EARLY)
+    near, far = pack(me, coeffs, EARLY)
+    tables, picks = fetch(me, tables, pattern, tiles)
     planes = len(far)
     far = [across(far[s], s * NEAR) for s in in_turn(planes)]
     near = [across(near[d], d) for d in in_turn(NEAR)]

time: 36.9 us -> 36.6 us (level)
  transfers between devices with their start and end apart: 10 -> 10, of which waited for: 5 -> 5; matrix products, arithmetic and copies ran while one was open for 0% -> 0% of each run, Pallas kernels for 13% -> 14%
where the time goes in v5:
time: 36.6 us; the launch traced here: 36.4 us
  starting transfers between devices  15.9 us (43%)
  Pallas kernels  11.6 us (32%)
  waiting for transfers between devices  8.85 us (24%)
    ppermute x9, starting transfers between devices, across(): return lax.ppermute(block, 'box', [(i, i ^ distance) for i in range(count)])  11.3 us
    ppermute x9, waiting for transfers between devices, across(): return lax.ppermute(block, 'box', [(i, i ^ distance) for i in range(count)])  7.34 us
    pallas_call x1, Pallas kernels, run_last(): pl.pallas_call(last_kernel, out_shape=jax.ShapeDtypeStruct((early + more,...  4.84 us
    all_to_all x1, starting transfers between devices, body(): lax.all_to_all(late_blocks(near), 'box', 0, 0, tiled=True, axis_index_gro...  4.62 us
    pallas_call x1, Pallas kernels, run_first(): pl.pallas_call(first_kernel, out_shape=jax.ShapeDtypeStruct((rhs, rank, t...  4.13 us
    all_to_all x1, waiting for transfers between devices, body(): lax.all_to_all(late_blocks(near), 'box', 0, 0, tiled=True, axis_index_gro...  1.51 us
    pallas_call x1, Pallas kernels, pack(): pl.pallas_call(functools.partial(pack_kernel, early), out_shape=[jax.Shap...  1.47 us
    pallas_call x1, Pallas kernels, late_blocks(): pl.pallas_call(late_kernel, out_shape=jax.ShapeDtypeStruct((planes, len(n...  0.83 us
  transfers between devices with their start and end apart: 10, of which 5 were waited for; matrix products, arithmetic and copies ran while one was open for 0% of the time, Pallas kernels for 14%

profile of v5, /device:TPU:0, one launch (start us, length us, event | category | flops | bytes accessed | tf_op | source)
XLA Modules:
  0.0 36.4 jit_solution(6808506189076712161)
XLA Ops:
  0.0 1.5 %shard_map.47 = (bf16[4,2,64,128]{3,2,1,0:T(8,128)(2,1)S(1)}, bf16[4,2,64,128]{3,2,1,0:T(8,128)(2,1)S(1)}, bf16[4,2,64,128]{3,2,1,0:T(8,128)(2,1)S(1)}, bf16[4,2...) custom-call(s32[1]{0:T(128)} %bitcast.me, ...), custom_call_target="tpu_custom_call" | custom-call | tf_op jit(solution)/shard_map/pallas_call | solution.py:53
  1.5 3.0 %collective-permute-start.6 = (bf16[4,2,64,128]{3,2,1,0:T(8,128)(2,1)S(1)}, bf16[4,2,64,128]{3,2,1,0:T(8,128)(2,1)S(1)}, u32[]{:S(2)}, u32[]{:S(2)}) collective-permute-start(bf16[4,2,64,128]{3,2,1,0:T(8,128)(2,1)S(1)} %get-tuple-element.30), channel_id=1, source_target_pairs={{0,2},{1,3},{2,0},{3,1},{4,6},{5,7},{6,4},{7,5},{8,10},{9,11},{10,... | collective-permute-start | bytes 393224 | tf_op jit(solution)/shard_map/ppermute | solution.py:258
  4.5 0.0 collective-permute-start.7
  4.5 0.2 collective-permute-start.8
  4.7 3.0 %collective-permute-start = (bf16[4,2,64,128]{3,2,1,0:T(8,128)(2,1)S(1)}, bf16[4,2,64,128]{3,2,1,0:T(8,128)(2,1)S(1)}, u32[]{:S(2)}, u32[]{:S(2)}) collective-permute-start(bf16[4,2,64,128]{3,2,1,0:T(8,128)(2,1)S(1)} %get-tuple-element.22), channel_id=1, source_target_pairs={{0,8},{1,9},{2,10},{3,11},{4,12},{5,13},{6,14},{7,15},{8,0},{9,1},... | collective-permute-start | bytes 393224 | tf_op jit(solution)/shard_map/ppermute | solution.py:258
  7.7 1.3 %collective-permute-start.1 = (bf16[4,2,64,128]{3,2,1,0:T(8,128)(2,1)S(1)}, bf16[4,2,64,128]{3,2,1,0:T(8,128)(2,1)S(1)}, u32[]{:S(2)}, u32[]{:S(2)}) collective-permute-start(bf16[4,2,64,128]{3,2,1,0:T(8,128)(2,1)S(1)} %get-tuple-element.23), channel_id=1, source_target_pairs={{0,12},{1,13},{2,14},{3,15},{4,8},{5,9},{6,10},{7,11},{8,4},{9,5},... | collective-permute-start | bytes 393224 | tf_op jit(solution)/shard_map/ppermute | solution.py:258
  9.1 0.0 collective-permute-done.6.refs_1_
  9.1 1.5 %collective-permute-start.2 = (bf16[4,2,64,128]{3,2,1,0:T(8,128)(2,1)S(1)}, bf16[4,2,64,128]{3,2,1,0:T(8,128)(2,1)S(1)}, u32[]{:S(2)}, u32[]{:S(2)}) collective-permute-start(bf16[4,2,64,128]{3,2,1,0:T(8,128)(2,1)S(1)} %get-tuple-element.24), channel_id=1, source_target_pairs={{0,4},{1,5},{2,6},{3,7},{4,0},{5,1},{6,2},{7,3},{8,12},{9,13},{10,... | collective-permute-start | bytes 393224 | tf_op jit(solution)/shard_map/ppermute | solution.py:258
  10.5 0.0 collective-permute-done.7.refs_2_
  10.5 0.0 collective-permute-done.8.refs_3_
  10.6 0.8 %shard_map.50 = bf16[4,4,2,64,128]{4,3,2,1,0:T(8,128)(2,1)} custom-call(bf16[4,2,64,128]{3,2,1,0:T(8,128)(2,1)S(1)} %get-tuple-element.29.refs_0_, bf16[4,2,64,128]{3,2,1,0:T(8,128)(2,1)S(1)} %collective-permute-done.6.refs_1_, bf16[4,2,64,128]{3,2,1,0:T(8,128)(2,1)S(1)} %collective-permute-done.7.refs_2_, ...), custom_call_target="tpu_custom_call" | custom-call | tf_op jit(solution)/shard_map/pallas_call | solution.py:101
  11.4 4.6 %all-to-all-start = ((bf16[4,4,2,64,128]{4,3,2,1,0:T(8,128)(2,1)}), bf16[4,4,2,64,128]{4,3,2,1,0:T(8,128)(2,1)S(1)}, u32[]{:S(2)}, u32[]{:S(2)}) async-start(bf16[4,4,2,64,128]{4,3,2,1,0:T(8,128)(2,1)} %shard_map.50), calls=%async_computation | async-start | bytes 1048576 | tf_op jit(solution)/shard_map/all_to_all | solution.py:288
  16.0 1.7 %collective-permute-done.refs_1_ = bf16[4,2,64,128]{3,2,1,0:T(8,128)(2,1)S(1)} collective-permute-done((bf16[4,2,64,128]{3,2,1,0:T(8,128)(2,1)S(1)}, bf16[4,2,64,128]{3,2,1,0:T(8,128)(2,1)S(1)}, u32[]{:S(2)}, u32[]{:S(2)}) %collective-permute-start) | collective-permute-done | bytes 131104 | tf_op jit(solution)/shard_map/ppermute | solution.py:258
  17.7 0.0 collective-permute-done.1.refs_2_
  17.7 0.7 %collective-permute-done.2.refs_3_ = bf16[4,2,64,128]{3,2,1,0:T(8,128)(2,1)S(1)} collective-permute-done((bf16[4,2,64,128]{3,2,1,0:T(8,128)(2,1)S(1)}, bf16[4,2,64,128]{3,2,1,0:T(8,128)(2,1)S(1)}, u32[]{:S(2)}, u32[]{:S(2)}) %collective-permute-start.2) | collective-permute-done | bytes 131104 | tf_op jit(solution)/shard_map/ppermute | solution.py:258
  18.4 0.0 copy-start
  18.4 0.0 copy-start.1
  18.4 1.6 %collective-permute-start.3 = (bf16[4,2,64,128]{3,2,1,0:T(8,128)(2,1)S(1)}, bf16[4,2,64,128]{3,2,1,0:T(8,128)(2,1)S(1)}, u32[]{:S(2)}, u32[]{:S(2)}) collective-permute-start(bf16[4,2,64,128]{3,2,1,0:T(8,128)(2,1)S(1)} %get-tuple-element.26), channel_id=1, source_target_pairs={{0,2},{1,3},{2,0},{3,1},{4,6},{5,7},{6,4},{7,5},{8,10},{9,11},{10,... | collective-permute-start | bytes 393224 | tf_op jit(solution)/shard_map/ppermute | solution.py:258
  20.1 0.0 collective-permute-start.4
  20.1 0.6 %collective-permute-start.5 = (bf16[4,2,64,128]{3,2,1,0:T(8,128)(2,1)S(1)}, bf16[4,2,64,128]{3,2,1,0:T(8,128)(2,1)S(1)}, u32[]{:S(2)}, u32[]{:S(2)}) collective-permute-start(bf16[4,2,64,128]{3,2,1,0:T(8,128)(2,1)S(1)} %get-tuple-element.28), channel_id=1, source_target_pairs={{0,1},{1,0},{2,3},{3,2},{4,5},{5,4},{6,7},{7,6},{8,9},{9,8},{10,11... | collective-permute-start | bytes 393224 | tf_op jit(solution)/shard_map/ppermute | solution.py:258
  20.6 0.0 copy-done
  20.6 0.0 copy-done.1
  20.6 0.0 copy-start.2
  20.6 0.3 shard_map.46
  20.9 3.0 %collective-permute-done.3.refs_1_ = bf16[4,2,64,128]{3,2,1,0:T(8,128)(2,1)S(1)} collective-permute-done((bf16[4,2,64,128]{3,2,1,0:T(8,128)(2,1)S(1)}, bf16[4,2,64,128]{3,2,1,0:T(8,128)(2,1)S(1)}, u32[]{:S(2)}, u32[]{:S(2)}) %collective-permute-start.3) | collective-permute-done | bytes 131104 | tf_op jit(solution)/shard_map/ppermute | solution.py:258
  23.9 2.0 %collective-permute-done.4.refs_2_ = bf16[4,2,64,128]{3,2,1,0:T(8,128)(2,1)S(1)} collective-permute-done((bf16[4,2,64,128]{3,2,1,0:T(8,128)(2,1)S(1)}, bf16[4,2,64,128]{3,2,1,0:T(8,128)(2,1)S(1)}, u32[]{:S(2)}, u32[]{:S(2)}) %collective-permute-start.4) | collective-permute-done | bytes 131104 | tf_op jit(solution)/shard_map/ppermute | solution.py:258
  25.9 0.0 collective-permute-done.5.refs_3_
  25.9 0.0 copy-done.2
  25.9 4.1 %shard_map.49.done = bf16[2,64,2048]{2,1,0:T(8,128)(2,1)S(1)} custom-call(s32[1]{0:T(128)} %bitcast.me, bf16[4,512,128]{2,1,0:T(8,128)(2,1)S(1)} %get-tuple-element.19.tables, s32[16,4,128]{2,1,0:T(4,128)S(1)} %get-tuple-element.20.picks, s32[1,2048]{1,0:T(1,128)S(1)} %bitcast.4, bf16[4,2,64,128]{3,2,1,0:T(8,128)(2,1)S(1)} %get-tuple-element.25.refs_0_, ...), custom_call_target="tpu_custom_call" | custom-call | flops 2000000000 | bytes 1024 | tf_op jit(solution)/shard_map/pallas_call | solution.py:206
  30.0 1.5 %all-to-all-done.late = bf16[4,4,2,64,128]{4,3,2,1,0:T(8,128)(2,1)S(1)} async-done(((bf16[4,4,2,64,128]{4,3,2,1,0:T(8,128)(2,1)}), bf16[4,4,2,64,128]{4,3,2,1,0:T(8,128)(2,1)S(1)}, u32[]{:S(2)}, u32[]{:S(2)}) %all-to-all-start) | async-done | bytes 524320 | tf_op jit(solution)/shard_map/all_to_all | solution.py:288
  31.5 4.8 %shard_map.51 = bf16[4,64,2048]{2,1,0:T(8,128)(2,1)} custom-call(s32[1]{0:T(128)} %bitcast.me, bf16[4,512,128]{2,1,0:T(8,128)(2,1)S(1)} %get-tuple-element.19.tables, s32[16,4,128]{2,1,0:T(4,128)S(1)} %get-tuple-element.20.picks, s32[1,2048]{1,0:T(1,128)S(1)} %bitcast.5, bf16[2,64,2048]{2,1,0:T(8,128)(2,1)S(1)} %shard_map.49.done, ...), custom_call_target="tpu_custom_call" | custom-call | flops 5000000000 | bytes 2097152 | tf_op jit(solution)/shard_map/pallas_call | solution.py:239
  (1 shorter events, 0.0 us)
Async XLA Ops:
  1.5 7.6 %collective-permute-start.6 = (bf16[4,2,64,128]{3,2,1,0:T(8,128)(2,1)S(1)}, bf16[4,2,64,128]{3,2,1,0:T(8,128)(2,1)S(1)}, u32[]{:S(2)}, u32[]{:S(2)}) collective-permute-start(bf16[4,2,64,128]{3,2,1,0:T(8,128)(2,1)S(1)} %get-tuple-element.30), channel_id=1, source_target_pairs={{0,2},{1,3},{2,0},{3,1},{4,6},{5,7},{6,4},{7,5},{8,10},{9,11},{10,... | collective-permute-start | bytes 393224 | tf_op jit(solution)/shard_map/ppermute | solution.py:258
  4.5 6.0 %collective-permute-start.7 = (bf16[4,2,64,128]{3,2,1,0:T(8,128)(2,1)S(1)}, bf16[4,2,64,128]{3,2,1,0:T(8,128)(2,1)S(1)}, u32[]{:S(2)}, u32[]{:S(2)}) collective-permute-start(bf16[4,2,64,128]{3,2,1,0:T(8,128)(2,1)S(1)} %get-tuple-element.31), channel_id=1, source_target_pairs={{0,3},{1,2},{2,1},{3,0},{4,7},{5,6},{6,5},{7,4},{8,11},{9,10},{10,... | collective-permute-start | bytes 393224 | tf_op jit(solution)/shard_map/ppermute | solution.py:258
  4.5 6.0 %collective-permute-start.8 = (bf16[4,2,64,128]{3,2,1,0:T(8,128)(2,1)S(1)}, bf16[4,2,64,128]{3,2,1,0:T(8,128)(2,1)S(1)}, u32[]{:S(2)}, u32[]{:S(2)}) collective-permute-start(bf16[4,2,64,128]{3,2,1,0:T(8,128)(2,1)S(1)} %get-tuple-element.32), channel_id=1, source_target_pairs={{0,1},{1,0},{2,3},{3,2},{4,5},{5,4},{6,7},{7,6},{8,9},{9,8},{10,11... | collective-permute-start | bytes 393224 | tf_op jit(solution)/shard_map/ppermute | solution.py:258
  4.7 13.0 %collective-permute-start = (bf16[4,2,64,128]{3,2,1,0:T(8,128)(2,1)S(1)}, bf16[4,2,64,128]{3,2,1,0:T(8,128)(2,1)S(1)}, u32[]{:S(2)}, u32[]{:S(2)}) collective-permute-start(bf16[4,2,64,128]{3,2,1,0:T(8,128)(2,1)S(1)} %get-tuple-element.22), channel_id=1, source_target_pairs={{0,8},{1,9},{2,10},{3,11},{4,12},{5,13},{6,14},{7,15},{8,0},{9,1},... | collective-permute-start | bytes 393224 | tf_op jit(solution)/shard_map/ppermute | solution.py:258
  7.7 10.0 %collective-permute-start.1 = (bf16[4,2,64,128]{3,2,1,0:T(8,128)(2,1)S(1)}, bf16[4,2,64,128]{3,2,1,0:T(8,128)(2,1)S(1)}, u32[]{:S(2)}, u32[]{:S(2)}) collective-permute-start(bf16[4,2,64,128]{3,2,1,0:T(8,128)(2,1)S(1)} %get-tuple-element.23), channel_id=1, source_target_pairs={{0,12},{1,13},{2,14},{3,15},{4,8},{5,9},{6,10},{7,11},{8,4},{9,5},... | collective-permute-start | bytes 393224 | tf_op jit(solution)/shard_map/ppermute | solution.py:258
  9.1 9.3 %collective-permute-start.2 = (bf16[4,2,64,128]{3,2,1,0:T(8,128)(2,1)S(1)}, bf16[4,2,64,128]{3,2,1,0:T(8,128)(2,1)S(1)}, u32[]{:S(2)}, u32[]{:S(2)}) collective-permute-start(bf16[4,2,64,128]{3,2,1,0:T(8,128)(2,1)S(1)} %get-tuple-element.24), channel_id=1, source_target_pairs={{0,4},{1,5},{2,6},{3,7},{4,0},{5,1},{6,2},{7,3},{8,12},{9,13},{10,... | collective-permute-start | bytes 393224 | tf_op jit(solution)/shard_map/ppermute | solution.py:258
  11.4 20.1 %all-to-all-start = ((bf16[4,4,2,64,128]{4,3,2,1,0:T(8,128)(2,1)}), bf16[4,4,2,64,128]{4,3,2,1,0:T(8,128)(2,1)S(1)}, u32[]{:S(2)}, u32[]{:S(2)}) async-start(bf16[4,4,2,64,128]{4,3,2,1,0:T(8,128)(2,1)} %shard_map.50), calls=%async_computation | async-start | bytes 1048576 | tf_op jit(solution)/shard_map/all_to_all | solution.py:288
  18.4 2.3 %copy-start = (bf16[4,8,64,128]{3,2,1,0:T(8,128)(2,1)S(1)}, bf16[4,8,64,128]{3,2,1,0:T(8,128)(2,1)}, u32[]{:S(2)}) copy-start(bf16[4,8,64,128]{3,2,1,0:T(8,128)(2,1)} %param.5) | copy-start | bytes 1572868
  18.4 2.3 %copy-start.1 = (s32[4,32768]{1,0:T(4,128)S(1)}, s32[4,32768]{1,0:T(4,128)}, u32[]{:S(2)}) copy-start(s32[4,32768]{1,0:T(4,128)} %pattern.1) | copy-start | bytes 1572868
  18.4 5.4 %collective-permute-start.3 = (bf16[4,2,64,128]{3,2,1,0:T(8,128)(2,1)S(1)}, bf16[4,2,64,128]{3,2,1,0:T(8,128)(2,1)S(1)}, u32[]{:S(2)}, u32[]{:S(2)}) collective-permute-start(bf16[4,2,64,128]{3,2,1,0:T(8,128)(2,1)S(1)} %get-tuple-element.26), channel_id=1, source_target_pairs={{0,2},{1,3},{2,0},{3,1},{4,6},{5,7},{6,4},{7,5},{8,10},{9,11},{10,... | collective-permute-start | bytes 393224 | tf_op jit(solution)/shard_map/ppermute | solution.py:258
  20.1 5.8 %collective-permute-start.4 = (bf16[4,2,64,128]{3,2,1,0:T(8,128)(2,1)S(1)}, bf16[4,2,64,128]{3,2,1,0:T(8,128)(2,1)S(1)}, u32[]{:S(2)}, u32[]{:S(2)}) collective-permute-start(bf16[4,2,64,128]{3,2,1,0:T(8,128)(2,1)S(1)} %get-tuple-element.27), channel_id=1, source_target_pairs={{0,3},{1,2},{2,1},{3,0},{4,7},{5,6},{6,5},{7,4},{8,11},{9,10},{10,... | collective-permute-start | bytes 393224 | tf_op jit(solution)/shard_map/ppermute | solution.py:258
  20.1 5.8 %collective-permute-start.5 = (bf16[4,2,64,128]{3,2,1,0:T(8,128)(2,1)S(1)}, bf16[4,2,64,128]{3,2,1,0:T(8,128)(2,1)S(1)}, u32[]{:S(2)}, u32[]{:S(2)}) collective-permute-start(bf16[4,2,64,128]{3,2,1,0:T(8,128)(2,1)S(1)} %get-tuple-element.28), channel_id=1, source_target_pairs={{0,1},{1,0},{2,3},{3,2},{4,5},{5,4},{6,7},{7,6},{8,9},{9,8},{10,11... | collective-permute-start | bytes 393224 | tf_op jit(solution)/shard_map/ppermute | solution.py:258
  20.6 5.2 %copy-start.2 = (s32[2048]{0:T(1024)S(1)}, s32[2048]{0:T(1024)}, u32[]{:S(2)}) copy-start(s32[2048]{0:T(1024)} %param.7) | copy-start | bytes 24580

commit v6 on v5

--- a/solution.py
+++ b/solution.py
@@ -140,17 +140,17 @@
                 [jnp.concatenate([before(tile, r) for tile in pair], axis=0) for r in range(rhs)], axis=1
             )
             product = jnp.dot(tables[level], joined, preferred_element_type=jnp.float32)
-            product = product.reshape(table_count, rank // 8, 8, rhs * LANES)
+            product = product.astype(jnp.bfloat16).reshape(table_count, rank // 16, 16, rhs * LANES)
             for tile in pair:
-                pick = jnp.broadcast_to(picks[tile, level : level + 1, :], (8, LANES))
+                pick = jnp.broadcast_to(picks[tile, level : level + 1, :], (16, LANES)).astype(jnp.int16)
                 pick = jnp.concatenate([pick] * rhs, axis=1)
                 choices = [product[t] for t in range(table_count)]
                 bit = 1
                 while len(choices) > 1:
-                    odd = (pick & bit) != 0
+                    odd = (pick & jnp.int16(bit)) != jnp.int16(0)
                     choices = [jnp.where(odd, b, a) for a, b in zip(choices[::2], choices[1::2])]
                     bit *= 2
-                chosen = choices[0].reshape(rank, rhs * LANES).astype(jnp.bfloat16)
+                chosen = choices[0].reshape(rank, rhs * LANES)
                 for r in range(rhs):
                     state[tile, r] = chosen[:, r * LANES : (r + 1) * LANES]
 
@@ -218,10 +218,9 @@
     early, rhs = done.shape[0], out.shape[0]
     copies = [pltpu.make_async_copy(done, out.at[0:early], sem.at[0])]
     copies[0].start()
-    for z in range(late.shape[0]):
-        for d in range(NEAR):
-            state[z * NEAR + ((me[0] % NEAR) ^ d)] = late[z, d]
-    all_levels(lambda tile, r: state[tile, r], tables, picks, state, state.shape[1])
+    own = me[0] % NEAR
+    arrived = lambda tile, r: late[tile // NEAR, (tile % NEAR) ^ own, r]
+    all_levels(arrived, tables, picks, state, state.shape[1])
     flat = flat_rows(state)
     for number, start in enumerate(range(0, out.shape[2], STRIP)):
         columns = slice(start, start + STRIP)

time: 36.6 us -> 36.4 us (level)
  Pallas kernels: 11.6 us -> 11.1 us
where the time goes in v6:
time: 36.4 us; the launch traced here: 36.1 us
  starting transfers between devices  15.9 us (44%)
  Pallas kernels  11.1 us (30%)
  waiting for transfers between devices  9.04 us (25%)
    ppermute x9, starting transfers between devices, across(): return lax.ppermute(block, 'box', [(i, i ^ distance) for i in range(count)])  11.3 us
    ppermute x9, waiting for transfers between devices, across(): return lax.ppermute(block, 'box', [(i, i ^ distance) for i in range(count)])  7.34 us
    all_to_all x1, starting transfers between devices, body(): lax.all_to_all(late_blocks(near), 'box', 0, 0, tiled=True, axis_index_gro...  4.62 us
    pallas_call x1, Pallas kernels, run_last(): pl.pallas_call(last_kernel, out_shape=jax.ShapeDtypeStruct((early + more,...  4.59 us
    pallas_call x1, Pallas kernels, run_first(): pl.pallas_call(first_kernel, out_shape=jax.ShapeDtypeStruct((rhs, rank, t...  3.94 us
    all_to_all x1, waiting for transfers between devices, body(): lax.all_to_all(late_blocks(near), 'box', 0, 0, tiled=True, axis_index_gro...  1.7 us
    pallas_call x1, Pallas kernels, pack(): pl.pallas_call(functools.partial(pack_kernel, early), out_shape=[jax.Shap...  1.47 us
    pallas_call x1, Pallas kernels, late_blocks(): pl.pallas_call(late_kernel, out_shape=jax.ShapeDtypeStruct((planes, len(n...  0.83 us
  transfers between devices with their start and end apart: 10, of which 5 were waited for; matrix products, arithmetic and copies ran while one was open for 0% of the time, Pallas kernels for 14%

profile of v6, /device:TPU:0, one launch (start us, length us, event | category | flops | bytes accessed | tf_op | source)
XLA Modules:
  0.0 36.1 jit_solution(17998328602678575235)
XLA Ops:
  0.0 1.5 %shard_map.47 = (bf16[4,2,64,128]{3,2,1,0:T(8,128)(2,1)S(1)}, bf16[4,2,64,128]{3,2,1,0:T(8,128)(2,1)S(1)}, bf16[4,2,64,128]{3,2,1,0:T(8,128)(2,1)S(1)}, bf16[4,2...) custom-call(s32[1]{0:T(128)} %bitcast.me, ...), custom_call_target="tpu_custom_call" | custom-call | tf_op jit(solution)/shard_map/pallas_call | solution.py:53
  1.5 3.0 %collective-permute-start.6 = (bf16[4,2,64,128]{3,2,1,0:T(8,128)(2,1)S(1)}, bf16[4,2,64,128]{3,2,1,0:T(8,128)(2,1)S(1)}, u32[]{:S(2)}, u32[]{:S(2)}) collective-permute-start(bf16[4,2,64,128]{3,2,1,0:T(8,128)(2,1)S(1)} %get-tuple-element.30), channel_id=1, source_target_pairs={{0,2},{1,3},{2,0},{3,1},{4,6},{5,7},{6,4},{7,5},{8,10},{9,11},{10,... | collective-permute-start | bytes 393224 | tf_op jit(solution)/shard_map/ppermute | solution.py:257
  4.5 0.0 collective-permute-start.7
  4.5 0.2 collective-permute-start.8
  4.7 3.0 %collective-permute-start = (bf16[4,2,64,128]{3,2,1,0:T(8,128)(2,1)S(1)}, bf16[4,2,64,128]{3,2,1,0:T(8,128)(2,1)S(1)}, u32[]{:S(2)}, u32[]{:S(2)}) collective-permute-start(bf16[4,2,64,128]{3,2,1,0:T(8,128)(2,1)S(1)} %get-tuple-element.22), channel_id=1, source_target_pairs={{0,8},{1,9},{2,10},{3,11},{4,12},{5,13},{6,14},{7,15},{8,0},{9,1},... | collective-permute-start | bytes 393224 | tf_op jit(solution)/shard_map/ppermute | solution.py:257
  7.7 1.3 %collective-permute-start.1 = (bf16[4,2,64,128]{3,2,1,0:T(8,128)(2,1)S(1)}, bf16[4,2,64,128]{3,2,1,0:T(8,128)(2,1)S(1)}, u32[]{:S(2)}, u32[]{:S(2)}) collective-permute-start(bf16[4,2,64,128]{3,2,1,0:T(8,128)(2,1)S(1)} %get-tuple-element.23), channel_id=1, source_target_pairs={{0,12},{1,13},{2,14},{3,15},{4,8},{5,9},{6,10},{7,11},{8,4},{9,5},... | collective-permute-start | bytes 393224 | tf_op jit(solution)/shard_map/ppermute | solution.py:257
  9.1 0.0 collective-permute-done.6.refs_1_
  9.1 1.5 %collective-permute-start.2 = (bf16[4,2,64,128]{3,2,1,0:T(8,128)(2,1)S(1)}, bf16[4,2,64,128]{3,2,1,0:T(8,128)(2,1)S(1)}, u32[]{:S(2)}, u32[]{:S(2)}) collective-permute-start(bf16[4,2,64,128]{3,2,1,0:T(8,128)(2,1)S(1)} %get-tuple-element.24), channel_id=1, source_target_pairs={{0,4},{1,5},{2,6},{3,7},{4,0},{5,1},{6,2},{7,3},{8,12},{9,13},{10,... | collective-permute-start | bytes 393224 | tf_op jit(solution)/shard_map/ppermute | solution.py:257
  10.5 0.0 collective-permute-done.7.refs_2_
  10.5 0.0 collective-permute-done.8.refs_3_
  10.6 0.8 %shard_map.50 = bf16[4,4,2,64,128]{4,3,2,1,0:T(8,128)(2,1)} custom-call(bf16[4,2,64,128]{3,2,1,0:T(8,128)(2,1)S(1)} %get-tuple-element.29.refs_0_, bf16[4,2,64,128]{3,2,1,0:T(8,128)(2,1)S(1)} %collective-permute-done.6.refs_1_, bf16[4,2,64,128]{3,2,1,0:T(8,128)(2,1)S(1)} %collective-permute-done.7.refs_2_, ...), custom_call_target="tpu_custom_call" | custom-call | tf_op jit(solution)/shard_map/pallas_call | solution.py:101
  11.4 4.6 %all-to-all-start = ((bf16[4,4,2,64,128]{4,3,2,1,0:T(8,128)(2,1)}), bf16[4,4,2,64,128]{4,3,2,1,0:T(8,128)(2,1)S(1)}, u32[]{:S(2)}, u32[]{:S(2)}) async-start(bf16[4,4,2,64,128]{4,3,2,1,0:T(8,128)(2,1)} %shard_map.50), calls=%async_computation | async-start | bytes 1048576 | tf_op jit(solution)/shard_map/all_to_all | solution.py:287
  16.0 1.7 %collective-permute-done.refs_1_ = bf16[4,2,64,128]{3,2,1,0:T(8,128)(2,1)S(1)} collective-permute-done((bf16[4,2,64,128]{3,2,1,0:T(8,128)(2,1)S(1)}, bf16[4,2,64,128]{3,2,1,0:T(8,128)(2,1)S(1)}, u32[]{:S(2)}, u32[]{:S(2)}) %collective-permute-start) | collective-permute-done | bytes 131104 | tf_op jit(solution)/shard_map/ppermute | solution.py:257
  17.7 0.0 collective-permute-done.1.refs_2_
  17.7 0.7 %collective-permute-done.2.refs_3_ = bf16[4,2,64,128]{3,2,1,0:T(8,128)(2,1)S(1)} collective-permute-done((bf16[4,2,64,128]{3,2,1,0:T(8,128)(2,1)S(1)}, bf16[4,2,64,128]{3,2,1,0:T(8,128)(2,1)S(1)}, u32[]{:S(2)}, u32[]{:S(2)}) %collective-permute-start.2) | collective-permute-done | bytes 131104 | tf_op jit(solution)/shard_map/ppermute | solution.py:257
  18.4 0.0 copy-start
  18.4 0.0 copy-start.1
  18.4 1.6 %collective-permute-start.3 = (bf16[4,2,64,128]{3,2,1,0:T(8,128)(2,1)S(1)}, bf16[4,2,64,128]{3,2,1,0:T(8,128)(2,1)S(1)}, u32[]{:S(2)}, u32[]{:S(2)}) collective-permute-start(bf16[4,2,64,128]{3,2,1,0:T(8,128)(2,1)S(1)} %get-tuple-element.26), channel_id=1, source_target_pairs={{0,2},{1,3},{2,0},{3,1},{4,6},{5,7},{6,4},{7,5},{8,10},{9,11},{10,... | collective-permute-start | bytes 393224 | tf_op jit(solution)/shard_map/ppermute | solution.py:257
  20.1 0.0 collective-permute-start.4
  20.1 0.6 %collective-permute-start.5 = (bf16[4,2,64,128]{3,2,1,0:T(8,128)(2,1)S(1)}, bf16[4,2,64,128]{3,2,1,0:T(8,128)(2,1)S(1)}, u32[]{:S(2)}, u32[]{:S(2)}) collective-permute-start(bf16[4,2,64,128]{3,2,1,0:T(8,128)(2,1)S(1)} %get-tuple-element.28), channel_id=1, source_target_pairs={{0,1},{1,0},{2,3},{3,2},{4,5},{5,4},{6,7},{7,6},{8,9},{9,8},{10,11... | collective-permute-start | bytes 393224 | tf_op jit(solution)/shard_map/ppermute | solution.py:257
  20.6 0.0 copy-done
  20.6 0.0 copy-done.1
  20.6 0.0 copy-start.2
  20.6 0.3 shard_map.46
  20.9 3.0 %collective-permute-done.3.refs_1_ = bf16[4,2,64,128]{3,2,1,0:T(8,128)(2,1)S(1)} collective-permute-done((bf16[4,2,64,128]{3,2,1,0:T(8,128)(2,1)S(1)}, bf16[4,2,64,128]{3,2,1,0:T(8,128)(2,1)S(1)}, u32[]{:S(2)}, u32[]{:S(2)}) %collective-permute-start.3) | collective-permute-done | bytes 131104 | tf_op jit(solution)/shard_map/ppermute | solution.py:257
  23.9 2.0 %collective-permute-done.4.refs_2_ = bf16[4,2,64,128]{3,2,1,0:T(8,128)(2,1)S(1)} collective-permute-done((bf16[4,2,64,128]{3,2,1,0:T(8,128)(2,1)S(1)}, bf16[4,2,64,128]{3,2,1,0:T(8,128)(2,1)S(1)}, u32[]{:S(2)}, u32[]{:S(2)}) %collective-permute-start.4) | collective-permute-done | bytes 131104 | tf_op jit(solution)/shard_map/ppermute | solution.py:257
  25.9 0.0 collective-permute-done.5.refs_3_
  25.9 0.0 copy-done.2
  25.9 3.9 %shard_map.49.done = bf16[2,64,2048]{2,1,0:T(8,128)(2,1)S(1)} custom-call(s32[1]{0:T(128)} %bitcast.me, bf16[4,512,128]{2,1,0:T(8,128)(2,1)S(1)} %get-tuple-element.19.tables, s32[16,4,128]{2,1,0:T(4,128)S(1)} %get-tuple-element.20.picks, s32[1,2048]{1,0:T(1,128)S(1)} %bitcast.4, bf16[4,2,64,128]{3,2,1,0:T(8,128)(2,1)S(1)} %get-tuple-element.25.refs_0_, ...), custom_call_target="tpu_custom_call" | custom-call | flops 2000000000 | bytes 1024 | tf_op jit(solution)/shard_map/pallas_call | solution.py:206
  29.8 1.7 %all-to-all-done.late = bf16[4,4,2,64,128]{4,3,2,1,0:T(8,128)(2,1)S(1)} async-done(((bf16[4,4,2,64,128]{4,3,2,1,0:T(8,128)(2,1)}), bf16[4,4,2,64,128]{4,3,2,1,0:T(8,128)(2,1)S(1)}, u32[]{:S(2)}, u32[]{:S(2)}) %all-to-all-start) | async-done | bytes 524320 | tf_op jit(solution)/shard_map/all_to_all | solution.py:287
  31.5 4.6 %shard_map.51 = bf16[4,64,2048]{2,1,0:T(8,128)(2,1)} custom-call(s32[1]{0:T(128)} %bitcast.me, bf16[4,512,128]{2,1,0:T(8,128)(2,1)S(1)} %get-tuple-element.19.tables, s32[16,4,128]{2,1,0:T(4,128)S(1)} %get-tuple-element.20.picks, s32[1,2048]{1,0:T(1,128)S(1)} %bitcast.5, bf16[2,64,2048]{2,1,0:T(8,128)(2,1)S(1)} %shard_map.49.done, ...), custom_call_target="tpu_custom_call" | custom-call | flops 5000000000 | bytes 2097152 | tf_op jit(solution)/shard_map/pallas_call | solution.py:238
  (1 shorter events, 0.0 us)
Async XLA Ops:
  1.5 7.6 %collective-permute-start.6 = (bf16[4,2,64,128]{3,2,1,0:T(8,128)(2,1)S(1)}, bf16[4,2,64,128]{3,2,1,0:T(8,128)(2,1)S(1)}, u32[]{:S(2)}, u32[]{:S(2)}) collective-permute-start(bf16[4,2,64,128]{3,2,1,0:T(8,128)(2,1)S(1)} %get-tuple-element.30), channel_id=1, source_target_pairs={{0,2},{1,3},{2,0},{3,1},{4,6},{5,7},{6,4},{7,5},{8,10},{9,11},{10,... | collective-permute-start | bytes 393224 | tf_op jit(solution)/shard_map/ppermute | solution.py:257
  4.5 6.0 %collective-permute-start.7 = (bf16[4,2,64,128]{3,2,1,0:T(8,128)(2,1)S(1)}, bf16[4,2,64,128]{3,2,1,0:T(8,128)(2,1)S(1)}, u32[]{:S(2)}, u32[]{:S(2)}) collective-permute-start(bf16[4,2,64,128]{3,2,1,0:T(8,128)(2,1)S(1)} %get-tuple-element.31), channel_id=1, source_target_pairs={{0,3},{1,2},{2,1},{3,0},{4,7},{5,6},{6,5},{7,4},{8,11},{9,10},{10,... | collective-permute-start | bytes 393224 | tf_op jit(solution)/shard_map/ppermute | solution.py:257
  4.5 6.0 %collective-permute-start.8 = (bf16[4,2,64,128]{3,2,1,0:T(8,128)(2,1)S(1)}, bf16[4,2,64,128]{3,2,1,0:T(8,128)(2,1)S(1)}, u32[]{:S(2)}, u32[]{:S(2)}) collective-permute-start(bf16[4,2,64,128]{3,2,1,0:T(8,128)(2,1)S(1)} %get-tuple-element.32), channel_id=1, source_target_pairs={{0,1},{1,0},{2,3},{3,2},{4,5},{5,4},{6,7},{7,6},{8,9},{9,8},{10,11... | collective-permute-start | bytes 393224 | tf_op jit(solution)/shard_map/ppermute | solution.py:257
  4.7 13.0 %collective-permute-start = (bf16[4,2,64,128]{3,2,1,0:T(8,128)(2,1)S(1)}, bf16[4,2,64,128]{3,2,1,0:T(8,128)(2,1)S(1)}, u32[]{:S(2)}, u32[]{:S(2)}) collective-permute-start(bf16[4,2,64,128]{3,2,1,0:T(8,128)(2,1)S(1)} %get-tuple-element.22), channel_id=1, source_target_pairs={{0,8},{1,9},{2,10},{3,11},{4,12},{5,13},{6,14},{7,15},{8,0},{9,1},... | collective-permute-start | bytes 393224 | tf_op jit(solution)/shard_map/ppermute | solution.py:257
  7.7 10.0 %collective-permute-start.1 = (bf16[4,2,64,128]{3,2,1,0:T(8,128)(2,1)S(1)}, bf16[4,2,64,128]{3,2,1,0:T(8,128)(2,1)S(1)}, u32[]{:S(2)}, u32[]{:S(2)}) collective-permute-start(bf16[4,2,64,128]{3,2,1,0:T(8,128)(2,1)S(1)} %get-tuple-element.23), channel_id=1, source_target_pairs={{0,12},{1,13},{2,14},{3,15},{4,8},{5,9},{6,10},{7,11},{8,4},{9,5},... | collective-permute-start | bytes 393224 | tf_op jit(solution)/shard_map/ppermute | solution.py:257
  9.1 9.3 %collective-permute-start.2 = (bf16[4,2,64,128]{3,2,1,0:T(8,128)(2,1)S(1)}, bf16[4,2,64,128]{3,2,1,0:T(8,128)(2,1)S(1)}, u32[]{:S(2)}, u32[]{:S(2)}) collective-permute-start(bf16[4,2,64,128]{3,2,1,0:T(8,128)(2,1)S(1)} %get-tuple-element.24), channel_id=1, source_target_pairs={{0,4},{1,5},{2,6},{3,7},{4,0},{5,1},{6,2},{7,3},{8,12},{9,13},{10,... | collective-permute-start | bytes 393224 | tf_op jit(solution)/shard_map/ppermute | solution.py:257
  11.4 20.1 %all-to-all-start = ((bf16[4,4,2,64,128]{4,3,2,1,0:T(8,128)(2,1)}), bf16[4,4,2,64,128]{4,3,2,1,0:T(8,128)(2,1)S(1)}, u32[]{:S(2)}, u32[]{:S(2)}) async-start(bf16[4,4,2,64,128]{4,3,2,1,0:T(8,128)(2,1)} %shard_map.50), calls=%async_computation | async-start | bytes 1048576 | tf_op jit(solution)/shard_map/all_to_all | solution.py:287
  18.4 2.3 %copy-start = (bf16[4,8,64,128]{3,2,1,0:T(8,128)(2,1)S(1)}, bf16[4,8,64,128]{3,2,1,0:T(8,128)(2,1)}, u32[]{:S(2)}) copy-start(bf16[4,8,64,128]{3,2,1,0:T(8,128)(2,1)} %param.5) | copy-start | bytes 1572868
  18.4 2.3 %copy-start.1 = (s32[4,32768]{1,0:T(4,128)S(1)}, s32[4,32768]{1,0:T(4,128)}, u32[]{:S(2)}) copy-start(s32[4,32768]{1,0:T(4,128)} %pattern.1) | copy-start | bytes 1572868
  18.4 5.4 %collective-permute-start.3 = (bf16[4,2,64,128]{3,2,1,0:T(8,128)(2,1)S(1)}, bf16[4,2,64,128]{3,2,1,0:T(8,128)(2,1)S(1)}, u32[]{:S(2)}, u32[]{:S(2)}) collective-permute-start(bf16[4,2,64,128]{3,2,1,0:T(8,128)(2,1)S(1)} %get-tuple-element.26), channel_id=1, source_target_pairs={{0,2},{1,3},{2,0},{3,1},{4,6},{5,7},{6,4},{7,5},{8,10},{9,11},{10,... | collective-permute-start | bytes 393224 | tf_op jit(solution)/shard_map/ppermute | solution.py:257
  20.1 5.8 %collective-permute-start.4 = (bf16[4,2,64,128]{3,2,1,0:T(8,128)(2,1)S(1)}, bf16[4,2,64,128]{3,2,1,0:T(8,128)(2,1)S(1)}, u32[]{:S(2)}, u32[]{:S(2)}) collective-permute-start(bf16[4,2,64,128]{3,2,1,0:T(8,128)(2,1)S(1)} %get-tuple-element.27), channel_id=1, source_target_pairs={{0,3},{1,2},{2,1},{3,0},{4,7},{5,6},{6,5},{7,4},{8,11},{9,10},{10,... | collective-permute-start | bytes 393224 | tf_op jit(solution)/shard_map/ppermute | solution.py:257
  20.1 5.8 %collective-permute-start.5 = (bf16[4,2,64,128]{3,2,1,0:T(8,128)(2,1)S(1)}, bf16[4,2,64,128]{3,2,1,0:T(8,128)(2,1)S(1)}, u32[]{:S(2)}, u32[]{:S(2)}) collective-permute-start(bf16[4,2,64,128]{3,2,1,0:T(8,128)(2,1)S(1)} %get-tuple-element.28), channel_id=1, source_target_pairs={{0,1},{1,0},{2,3},{3,2},{4,5},{5,4},{6,7},{7,6},{8,9},{9,8},{10,11... | collective-permute-start | bytes 393224 | tf_op jit(solution)/shard_map/ppermute | solution.py:257
  20.6 5.2 %copy-start.2 = (s32[2048]{0:T(1024)S(1)}, s32[2048]{0:T(1024)}, u32[]{:S(2)}) copy-start(s32[2048]{0:T(1024)} %param.7) | copy-start | bytes 24580

commit v7 on v6

--- a/solution.py
+++ b/solution.py
@@ -23,6 +23,15 @@
 
 def in_turn(count):
     return [0] + list(range(max(count // 2, 1), count)) + list(range(1, count // 2))
+
+
+def mixed(count):
+    turns = in_turn(count)
+    far, close = turns[1 : 1 + count - max(count // 2, 1)], turns[1 + count - max(count // 2, 1) :]
+    order = [0]
+    for n in range(len(far)):
+        order += far[n : n + 1] + close[n : n + 1]
+    return order
 
 
 def pack_kernel(early, me, coeffs, *refs):
@@ -109,7 +118,7 @@
 
 def early_kernel(*refs):
     far, early = refs[:-NEAR], refs[-NEAR:]
-    for s, ref in zip(in_turn(len(far)), far):
+    for s, ref in zip(mixed(len(far)), far):
         for d in range(NEAR):
             early[d][s] = ref[d]
 
@@ -281,7 +290,7 @@
     near, far = pack(me, coeffs, EARLY)
     tables, picks = fetch(me, tables, pattern, tiles)
     planes = len(far)
-    far = [across(far[s], s * NEAR) for s in in_turn(planes)]
+    far = [across(far[s], s * NEAR) for s in mixed(planes)]
     near = [across(near[d], d) for d in in_turn(NEAR)]
     columns = [[z * NEAR + d for z in range(planes)] for d in range(NEAR)]
     late = lax.all_to_all(late_blocks(near), "box", 0, 0, tiled=True, axis_index_groups=columns)

time: 36.4 us -> 36.4 us (level)
  starting transfers between devices: 15.9 us -> 16.8 us
  waiting for transfers between devices: 9.04 us -> 8.15 us
    ppermute x9, starting transfers between devices: 11.3 us -> 13.3 us  [across(): return lax.ppermute(block, 'box', [(i, i ^ distance) for i in range(count)])]
    all_to_all x1, starting transfers between devices: 4.62 us -> 3.47 us  [body(): lax.all_to_all(late_blocks(near), 'box', 0, 0, tiled=True, axis_index_gro...]
    ppermute x9, waiting for transfers between devices: 7.34 us -> 6.22 us  [across(): return lax.ppermute(block, 'box', [(i, i ^ distance) for i in range(count)])]
  transfers between devices with their start and end apart: 10 -> 10, of which waited for: 5 -> 4; matrix products, arithmetic and copies ran while one was open for 0% -> 0% of each run, Pallas kernels for 14% -> 14%
where the time goes in v7:
time: 36.4 us; the launch traced here: 36.1 us
  starting transfers between devices  16.8 us (46%)
  Pallas kernels  11.1 us (30%)
  waiting for transfers between devices  8.15 us (22%)
    ppermute x9, starting transfers between devices, across(): return lax.ppermute(block, 'box', [(i, i ^ distance) for i in range(count)])  13.3 us
    ppermute x9, waiting for transfers between devices, across(): return lax.ppermute(block, 'box', [(i, i ^ distance) for i in range(count)])  6.22 us
    pallas_call x1, Pallas kernels, run_last(): pl.pallas_call(last_kernel, out_shape=jax.ShapeDtypeStruct((early + more,...  4.59 us
    pallas_call x1, Pallas kernels, run_first(): pl.pallas_call(first_kernel, out_shape=jax.ShapeDtypeStruct((rhs, rank, t...  3.94 us
    all_to_all x1, starting transfers between devices, body(): lax.all_to_all(late_blocks(near), 'box', 0, 0, tiled=True, axis_index_gro...  3.47 us
    all_to_all x1, waiting for transfers between devices, body(): lax.all_to_all(late_blocks(near), 'box', 0, 0, tiled=True, axis_index_gro...  1.93 us
    pallas_call x1, Pallas kernels, pack(): pl.pallas_call(functools.partial(pack_kernel, early), out_shape=[jax.Shap...  1.47 us
    pallas_call x1, Pallas kernels, late_blocks(): pl.pallas_call(late_kernel, out_shape=jax.ShapeDtypeStruct((planes, len(n...  0.83 us
  transfers between devices with their start and end apart: 10, of which 4 were waited for; matrix products, arithmetic and copies ran while one was open for 0% of the time, Pallas kernels for 14%

profile of v7, /device:TPU:0, one launch (start us, length us, event | category | flops | bytes accessed | tf_op | source)
XLA Modules:
  0.0 36.1 jit_solution(15082679510357700613)
XLA Ops:
  0.0 1.5 %shard_map.47 = (bf16[4,2,64,128]{3,2,1,0:T(8,128)(2,1)S(1)}, bf16[4,2,64,128]{3,2,1,0:T(8,128)(2,1)S(1)}, bf16[4,2,64,128]{3,2,1,0:T(8,128)(2,1)S(1)}, bf16[4,2...) custom-call(s32[1]{0:T(128)} %bitcast.me, ...), custom_call_target="tpu_custom_call" | custom-call | tf_op jit(solution)/shard_map/pallas_call | solution.py:62
  1.5 3.0 %collective-permute-start.6 = (bf16[4,2,64,128]{3,2,1,0:T(8,128)(2,1)S(1)}, bf16[4,2,64,128]{3,2,1,0:T(8,128)(2,1)S(1)}, u32[]{:S(2)}, u32[]{:S(2)}) collective-permute-start(bf16[4,2,64,128]{3,2,1,0:T(8,128)(2,1)S(1)} %get-tuple-element.30), channel_id=1, source_target_pairs={{0,2},{1,3},{2,0},{3,1},{4,6},{5,7},{6,4},{7,5},{8,10},{9,11},{10,... | collective-permute-start | bytes 393224 | tf_op jit(solution)/shard_map/ppermute | solution.py:266
  4.5 0.0 collective-permute-start.7
  4.5 0.2 collective-permute-start.8
  4.7 3.0 %collective-permute-start = (bf16[4,2,64,128]{3,2,1,0:T(8,128)(2,1)S(1)}, bf16[4,2,64,128]{3,2,1,0:T(8,128)(2,1)S(1)}, u32[]{:S(2)}, u32[]{:S(2)}) collective-permute-start(bf16[4,2,64,128]{3,2,1,0:T(8,128)(2,1)S(1)} %get-tuple-element.22), channel_id=1, source_target_pairs={{0,8},{1,9},{2,10},{3,11},{4,12},{5,13},{6,14},{7,15},{8,0},{9,1},... | collective-permute-start | bytes 393224 | tf_op jit(solution)/shard_map/ppermute | solution.py:266
  7.7 1.6 %collective-permute-start.1 = (bf16[4,2,64,128]{3,2,1,0:T(8,128)(2,1)S(1)}, bf16[4,2,64,128]{3,2,1,0:T(8,128)(2,1)S(1)}, u32[]{:S(2)}, u32[]{:S(2)}) collective-permute-start(bf16[4,2,64,128]{3,2,1,0:T(8,128)(2,1)S(1)} %get-tuple-element.23), channel_id=1, source_target_pairs={{0,4},{1,5},{2,6},{3,7},{4,0},{5,1},{6,2},{7,3},{8,12},{9,13},{10,... | collective-permute-start | bytes 393224 | tf_op jit(solution)/shard_map/ppermute | solution.py:266
  9.3 0.0 collective-permute-done.6.refs_1_
  9.3 3.3 %collective-permute-start.2 = (bf16[4,2,64,128]{3,2,1,0:T(8,128)(2,1)S(1)}, bf16[4,2,64,128]{3,2,1,0:T(8,128)(2,1)S(1)}, u32[]{:S(2)}, u32[]{:S(2)}) collective-permute-start(bf16[4,2,64,128]{3,2,1,0:T(8,128)(2,1)S(1)} %get-tuple-element.24), channel_id=1, source_target_pairs={{0,12},{1,13},{2,14},{3,15},{4,8},{5,9},{6,10},{7,11},{8,4},{9,5},... | collective-permute-start | bytes 393224 | tf_op jit(solution)/shard_map/ppermute | solution.py:266
  12.6 0.0 collective-permute-done.7.refs_2_
  12.6 0.0 collective-permute-done.8.refs_3_
  12.6 0.8 %shard_map.50 = bf16[4,4,2,64,128]{4,3,2,1,0:T(8,128)(2,1)} custom-call(bf16[4,2,64,128]{3,2,1,0:T(8,128)(2,1)S(1)} %get-tuple-element.29.refs_0_, bf16[4,2,64,128]{3,2,1,0:T(8,128)(2,1)S(1)} %collective-permute-done.6.refs_1_, bf16[4,2,64,128]{3,2,1,0:T(8,128)(2,1)S(1)} %collective-permute-done.7.refs_2_, ...), custom_call_target="tpu_custom_call" | custom-call | tf_op jit(solution)/shard_map/pallas_call | solution.py:110
  13.4 3.5 %all-to-all-start = ((bf16[4,4,2,64,128]{4,3,2,1,0:T(8,128)(2,1)}), bf16[4,4,2,64,128]{4,3,2,1,0:T(8,128)(2,1)S(1)}, u32[]{:S(2)}, u32[]{:S(2)}) async-start(bf16[4,4,2,64,128]{4,3,2,1,0:T(8,128)(2,1)} %shard_map.50), calls=%async_computation | async-start | bytes 1048576 | tf_op jit(solution)/shard_map/all_to_all | solution.py:296
  16.9 0.0 collective-permute-done.refs_1_
  16.9 0.0 collective-permute-done.1.refs_2_
  16.9 1.3 %collective-permute-done.2.refs_3_ = bf16[4,2,64,128]{3,2,1,0:T(8,128)(2,1)S(1)} collective-permute-done((bf16[4,2,64,128]{3,2,1,0:T(8,128)(2,1)S(1)}, bf16[4,2,64,128]{3,2,1,0:T(8,128)(2,1)S(1)}, u32[]{:S(2)}, u32[]{:S(2)}) %collective-permute-start.2) | collective-permute-done | bytes 131104 | tf_op jit(solution)/shard_map/ppermute | solution.py:266
  18.2 0.0 copy-start
  18.2 0.0 copy-start.1
  18.3 1.6 %collective-permute-start.3 = (bf16[4,2,64,128]{3,2,1,0:T(8,128)(2,1)S(1)}, bf16[4,2,64,128]{3,2,1,0:T(8,128)(2,1)S(1)}, u32[]{:S(2)}, u32[]{:S(2)}) collective-permute-start(bf16[4,2,64,128]{3,2,1,0:T(8,128)(2,1)S(1)} %get-tuple-element.26), channel_id=1, source_target_pairs={{0,2},{1,3},{2,0},{3,1},{4,6},{5,7},{6,4},{7,5},{8,10},{9,11},{10,... | collective-permute-start | bytes 393224 | tf_op jit(solution)/shard_map/ppermute | solution.py:266
  19.9 0.0 collective-permute-start.4
  19.9 0.6 %collective-permute-start.5 = (bf16[4,2,64,128]{3,2,1,0:T(8,128)(2,1)S(1)}, bf16[4,2,64,128]{3,2,1,0:T(8,128)(2,1)S(1)}, u32[]{:S(2)}, u32[]{:S(2)}) collective-permute-start(bf16[4,2,64,128]{3,2,1,0:T(8,128)(2,1)S(1)} %get-tuple-element.28), channel_id=1, source_target_pairs={{0,1},{1,0},{2,3},{3,2},{4,5},{5,4},{6,7},{7,6},{8,9},{9,8},{10,11... | collective-permute-start | bytes 393224 | tf_op jit(solution)/shard_map/ppermute | solution.py:266
  20.5 0.0 copy-done
  20.5 0.0 copy-done.1
  20.5 0.0 copy-start.2
  20.5 0.3 shard_map.46
  20.7 3.0 %collective-permute-done.3.refs_1_ = bf16[4,2,64,128]{3,2,1,0:T(8,128)(2,1)S(1)} collective-permute-done((bf16[4,2,64,128]{3,2,1,0:T(8,128)(2,1)S(1)}, bf16[4,2,64,128]{3,2,1,0:T(8,128)(2,1)S(1)}, u32[]{:S(2)}, u32[]{:S(2)}) %collective-permute-start.3) | collective-permute-done | bytes 131104 | tf_op jit(solution)/shard_map/ppermute | solution.py:266
  23.8 1.9 %collective-permute-done.4.refs_2_ = bf16[4,2,64,128]{3,2,1,0:T(8,128)(2,1)S(1)} collective-permute-done((bf16[4,2,64,128]{3,2,1,0:T(8,128)(2,1)S(1)}, bf16[4,2,64,128]{3,2,1,0:T(8,128)(2,1)S(1)}, u32[]{:S(2)}, u32[]{:S(2)}) %collective-permute-start.4) | collective-permute-done | bytes 131104 | tf_op jit(solution)/shard_map/ppermute | solution.py:266
  25.6 0.0 collective-permute-done.5.refs_3_
  25.6 0.0 copy-done.2
  25.6 3.9 %shard_map.49.done = bf16[2,64,2048]{2,1,0:T(8,128)(2,1)S(1)} custom-call(s32[1]{0:T(128)} %bitcast.me, bf16[4,512,128]{2,1,0:T(8,128)(2,1)S(1)} %get-tuple-element.19.tables, s32[16,4,128]{2,1,0:T(4,128)S(1)} %get-tuple-element.20.picks, s32[1,2048]{1,0:T(1,128)S(1)} %bitcast.4, bf16[4,2,64,128]{3,2,1,0:T(8,128)(2,1)S(1)} %get-tuple-element.25.refs_0_, ...), custom_call_target="tpu_custom_call" | custom-call | flops 2000000000 | bytes 1024 | tf_op jit(solution)/shard_map/pallas_call | solution.py:215
  29.6 1.9 %all-to-all-done.late = bf16[4,4,2,64,128]{4,3,2,1,0:T(8,128)(2,1)S(1)} async-done(((bf16[4,4,2,64,128]{4,3,2,1,0:T(8,128)(2,1)}), bf16[4,4,2,64,128]{4,3,2,1,0:T(8,128)(2,1)S(1)}, u32[]{:S(2)}, u32[]{:S(2)}) %all-to-all-start) | async-done | bytes 524320 | tf_op jit(solution)/shard_map/all_to_all | solution.py:296
  31.5 4.6 %shard_map.51 = bf16[4,64,2048]{2,1,0:T(8,128)(2,1)} custom-call(s32[1]{0:T(128)} %bitcast.me, bf16[4,512,128]{2,1,0:T(8,128)(2,1)S(1)} %get-tuple-element.19.tables, s32[16,4,128]{2,1,0:T(4,128)S(1)} %get-tuple-element.20.picks, s32[1,2048]{1,0:T(1,128)S(1)} %bitcast.5, bf16[2,64,2048]{2,1,0:T(8,128)(2,1)S(1)} %shard_map.49.done, ...), custom_call_target="tpu_custom_call" | custom-call | flops 5000000000 | bytes 2097152 | tf_op jit(solution)/shard_map/pallas_call | solution.py:247
  (1 shorter events, 0.0 us)
Async XLA Ops:
  1.5 7.8 %collective-permute-start.6 = (bf16[4,2,64,128]{3,2,1,0:T(8,128)(2,1)S(1)}, bf16[4,2,64,128]{3,2,1,0:T(8,128)(2,1)S(1)}, u32[]{:S(2)}, u32[]{:S(2)}) collective-permute-start(bf16[4,2,64,128]{3,2,1,0:T(8,128)(2,1)S(1)} %get-tuple-element.30), channel_id=1, source_target_pairs={{0,2},{1,3},{2,0},{3,1},{4,6},{5,7},{6,4},{7,5},{8,10},{9,11},{10,... | collective-permute-start | bytes 393224 | tf_op jit(solution)/shard_map/ppermute | solution.py:266
  4.5 8.1 %collective-permute-start.7 = (bf16[4,2,64,128]{3,2,1,0:T(8,128)(2,1)S(1)}, bf16[4,2,64,128]{3,2,1,0:T(8,128)(2,1)S(1)}, u32[]{:S(2)}, u32[]{:S(2)}) collective-permute-start(bf16[4,2,64,128]{3,2,1,0:T(8,128)(2,1)S(1)} %get-tuple-element.31), channel_id=1, source_target_pairs={{0,3},{1,2},{2,1},{3,0},{4,7},{5,6},{6,5},{7,4},{8,11},{9,10},{10,... | collective-permute-start | bytes 393224 | tf_op jit(solution)/shard_map/ppermute | solution.py:266
  4.5 8.1 %collective-permute-start.8 = (bf16[4,2,64,128]{3,2,1,0:T(8,128)(2,1)S(1)}, bf16[4,2,64,128]{3,2,1,0:T(8,128)(2,1)S(1)}, u32[]{:S(2)}, u32[]{:S(2)}) collective-permute-start(bf16[4,2,64,128]{3,2,1,0:T(8,128)(2,1)S(1)} %get-tuple-element.32), channel_id=1, source_target_pairs={{0,1},{1,0},{2,3},{3,2},{4,5},{5,4},{6,7},{7,6},{8,9},{9,8},{10,11... | collective-permute-start | bytes 393224 | tf_op jit(solution)/shard_map/ppermute | solution.py:266
  4.7 12.2 %collective-permute-start = (bf16[4,2,64,128]{3,2,1,0:T(8,128)(2,1)S(1)}, bf16[4,2,64,128]{3,2,1,0:T(8,128)(2,1)S(1)}, u32[]{:S(2)}, u32[]{:S(2)}) collective-permute-start(bf16[4,2,64,128]{3,2,1,0:T(8,128)(2,1)S(1)} %get-tuple-element.22), channel_id=1, source_target_pairs={{0,8},{1,9},{2,10},{3,11},{4,12},{5,13},{6,14},{7,15},{8,0},{9,1},... | collective-permute-start | bytes 393224 | tf_op jit(solution)/shard_map/ppermute | solution.py:266
  7.7 9.2 %collective-permute-start.1 = (bf16[4,2,64,128]{3,2,1,0:T(8,128)(2,1)S(1)}, bf16[4,2,64,128]{3,2,1,0:T(8,128)(2,1)S(1)}, u32[]{:S(2)}, u32[]{:S(2)}) collective-permute-start(bf16[4,2,64,128]{3,2,1,0:T(8,128)(2,1)S(1)} %get-tuple-element.23), channel_id=1, source_target_pairs={{0,4},{1,5},{2,6},{3,7},{4,0},{5,1},{6,2},{7,3},{8,12},{9,13},{10,... | collective-permute-start | bytes 393224 | tf_op jit(solution)/shard_map/ppermute | solution.py:266
  9.3 8.9 %collective-permute-start.2 = (bf16[4,2,64,128]{3,2,1,0:T(8,128)(2,1)S(1)}, bf16[4,2,64,128]{3,2,1,0:T(8,128)(2,1)S(1)}, u32[]{:S(2)}, u32[]{:S(2)}) collective-permute-start(bf16[4,2,64,128]{3,2,1,0:T(8,128)(2,1)S(1)} %get-tuple-element.24), channel_id=1, source_target_pairs={{0,12},{1,13},{2,14},{3,15},{4,8},{5,9},{6,10},{7,11},{8,4},{9,5},... | collective-permute-start | bytes 393224 | tf_op jit(solution)/shard_map/ppermute | solution.py:266
  13.4 18.1 %all-to-all-start = ((bf16[4,4,2,64,128]{4,3,2,1,0:T(8,128)(2,1)}), bf16[4,4,2,64,128]{4,3,2,1,0:T(8,128)(2,1)S(1)}, u32[]{:S(2)}, u32[]{:S(2)}) async-start(bf16[4,4,2,64,128]{4,3,2,1,0:T(8,128)(2,1)} %shard_map.50), calls=%async_computation | async-start | bytes 1048576 | tf_op jit(solution)/shard_map/all_to_all | solution.py:296
  18.2 2.3 %copy-start = (bf16[4,8,64,128]{3,2,1,0:T(8,128)(2,1)S(1)}, bf16[4,8,64,128]{3,2,1,0:T(8,128)(2,1)}, u32[]{:S(2)}) copy-start(bf16[4,8,64,128]{3,2,1,0:T(8,128)(2,1)} %param.5) | copy-start | bytes 1572868
  18.2 2.3 %copy-start.1 = (s32[4,32768]{1,0:T(4,128)S(1)}, s32[4,32768]{1,0:T(4,128)}, u32[]{:S(2)}) copy-start(s32[4,32768]{1,0:T(4,128)} %pattern.1) | copy-start | bytes 1572868
  18.3 5.5 %collective-permute-start.3 = (bf16[4,2,64,128]{3,2,1,0:T(8,128)(2,1)S(1)}, bf16[4,2,64,128]{3,2,1,0:T(8,128)(2,1)S(1)}, u32[]{:S(2)}, u32[]{:S(2)}) collective-permute-start(bf16[4,2,64,128]{3,2,1,0:T(8,128)(2,1)S(1)} %get-tuple-element.26), channel_id=1, source_target_pairs={{0,2},{1,3},{2,0},{3,1},{4,6},{5,7},{6,4},{7,5},{8,10},{9,11},{10,... | collective-permute-start | bytes 393224 | tf_op jit(solution)/shard_map/ppermute | solution.py:266
  19.9 5.8 %collective-permute-start.4 = (bf16[4,2,64,128]{3,2,1,0:T(8,128)(2,1)S(1)}, bf16[4,2,64,128]{3,2,1,0:T(8,128)(2,1)S(1)}, u32[]{:S(2)}, u32[]{:S(2)}) collective-permute-start(bf16[4,2,64,128]{3,2,1,0:T(8,128)(2,1)S(1)} %get-tuple-element.27), channel_id=1, source_target_pairs={{0,3},{1,2},{2,1},{3,0},{4,7},{5,6},{6,5},{7,4},{8,11},{9,10},{10,... | collective-permute-start | bytes 393224 | tf_op jit(solution)/shard_map/ppermute | solution.py:266
  19.9 5.8 %collective-permute-start.5 = (bf16[4,2,64,128]{3,2,1,0:T(8,128)(2,1)S(1)}, bf16[4,2,64,128]{3,2,1,0:T(8,128)(2,1)S(1)}, u32[]{:S(2)}, u32[]{:S(2)}) collective-permute-start(bf16[4,2,64,128]{3,2,1,0:T(8,128)(2,1)S(1)} %get-tuple-element.28), channel_id=1, source_target_pairs={{0,1},{1,0},{2,3},{3,2},{4,5},{5,4},{6,7},{7,6},{8,9},{9,8},{10,11... | collective-permute-start | bytes 393224 | tf_op jit(solution)/shard_map/ppermute | solution.py:266
  20.5 5.2 %copy-start.2 = (s32[2048]{0:T(1024)S(1)}, s32[2048]{0:T(1024)}, u32[]{:S(2)}) copy-start(s32[2048]{0:T(1024)} %param.7) | copy-start | bytes 24580
